TPU v7x, 512 devices: a whole 4x4x16 slice. The times are simulated.
512 devices in a mesh: dp: 32 (over x_lo, z), ctx: 16 (over y, x_hi, core).
Axes of the slice: x: 4 (x_hi: 2, x_lo: 2; x = x_hi * 2 + x_lo), y: 4, z: 16, core: 2. Of those that a mesh axis runs over, the one named last changes fastest.
Arguments:
- gate_out: bfloat16 [32, 512, 2048], P('dp', None, 'ctx'), may hold values from -6 to 6
- gate_in: bfloat16 [32, 512, 2048], P('dp', None, 'ctx'), may hold values from -6 to 6
- signal: bfloat16 [32, 512, 2048], P('dp', None, 'ctx'), may hold values from -6 to 6
- cotangent: bfloat16 [32, 512, 2048], P('dp', None, 'ctx'), may hold values from -6 to 6
- residue: float32 [32, 16], replicated, may hold values from -1 to 1
- decay: float32 [32, 16], replicated, may hold values from 0.25 to 64
- skip_bias: float32 [512], replicated, may hold values from -1 to 1
- channel_group: int32 [512], replicated, may hold values from 0 to 31, as said below
Outputs:
- conv_out: bfloat16 [32, 512, 2048], P('dp', None, 'ctx')
- grad_gate_out: bfloat16 [32, 512, 2048], P('dp', None, 'ctx')
- grad_gate_in: bfloat16 [32, 512, 2048], P('dp', None, 'ctx')
- grad_signal: bfloat16 [32, 512, 2048], P('dp', None, 'ctx')
- grad_filter: float32 [32, 2048], P(None, 'ctx')
- grad_residue: float32 [32, 16], replicated
- grad_bias: float32 [512], replicated
Inputs may be any that keep to these rules, and one draw needn't show every extreme that they name: `channel_group`: each of the 32 groups is named by exactly 16 channels.
All inputs are finite; a program needn't handle non-finite values.
Results may differ from a plain program's by a relative error of at most 0.01.
Values may be sent and summed in bfloat16 or wider, within the bound.
A program may use at most 64 MiB of HBM per device.

v0:
```python
import math

import jax
import jax.numpy as jnp
from jax import lax
from jax.sharding import PartitionSpec as P

GROUP_SIZE = 16


def dft_plan(total):
    second = 128
    first = total // 128
    rows = jnp.arange(first)
    cols = jnp.arange(second)
    angle_first = (
        2.0 * math.pi / first * (rows[:, None] * rows[None, :] % first).astype(jnp.float32)
    )
    angle_second = (
        2.0 * math.pi / second * (cols[:, None] * cols[None, :] % second).astype(jnp.float32)
    )
    angle_turn = 2.0 * math.pi / total * (rows[:, None] * cols[None, :] % total).astype(jnp.float32)
    return (
        first,
        second,
        jnp.cos(angle_first),
        jnp.sin(angle_first),
        jnp.cos(angle_second),
        jnp.sin(angle_second),
        jnp.cos(angle_turn),
        jnp.sin(angle_turn),
    )


def contract(form, left, right):
    return jnp.einsum(form, left, right, precision=lax.Precision.HIGHEST)


def forward_real(signals, plan):
    first, second, cos_first, sin_first, cos_second, sin_second, cos_turn, sin_turn = plan
    half = first // 2
    grid = signals.reshape(signals.shape[:-1] + (half, second))
    part_real = contract("pcij,ik->pckj", grid, cos_first[:half])
    part_imag = -contract("pcij,ik->pckj", grid, sin_first[:half])
    turned_real = part_real * cos_turn + part_imag * sin_turn
    turned_imag = part_imag * cos_turn - part_real * sin_turn
    spec_real = contract("pckj,jm->pckm", turned_real, cos_second) + contract(
        "pckj,jm->pckm", turned_imag, sin_second
    )
    spec_imag = contract("pckj,jm->pckm", turned_imag, cos_second) - contract(
        "pckj,jm->pckm", turned_real, sin_second
    )
    return (spec_real, spec_imag)


def inverse_real(spec_real, spec_imag, plan, total):
    first, second, cos_first, sin_first, cos_second, sin_second, cos_turn, sin_turn = plan
    back_real = contract("pckm,mj->pckj", spec_real, cos_second) - contract(
        "pckm,mj->pckj", spec_imag, sin_second
    )
    back_imag = contract("pckm,mj->pckj", spec_imag, cos_second) + contract(
        "pckm,mj->pckj", spec_real, sin_second
    )
    turned_real = back_real * cos_turn - back_imag * sin_turn
    turned_imag = back_imag * cos_turn + back_real * sin_turn
    half = first // 2
    values = contract("pckj,nk->pcnj", turned_real, cos_first[:half]) - contract(
        "pckj,nk->pcnj", turned_imag, sin_first[:half]
    )
    return values.reshape(values.shape[:2] + (half * second,)) / total


def body(gate_out, gate_in, signal, cotangent, residue, decay, skip_bias, channel_group):
    context_size = lax.axis_size("ctx")
    data_size = lax.axis_size("dp")
    context_index = lax.axis_index("ctx")
    channels = gate_out.shape[1]
    tok_rows = gate_out.shape[2]
    seq_len = tok_rows * context_size
    per_device = channels // context_size
    groups = residue.shape[0]
    mixed_in = (gate_in.astype(jnp.float32) * signal.astype(jnp.float32)).astype(jnp.bfloat16)
    back_grad = (cotangent.astype(jnp.float32) * gate_out.astype(jnp.float32)).astype(jnp.bfloat16)
    mixed_wide = mixed_in.astype(jnp.float32)
    back_wide = back_grad.astype(jnp.float32)
    bias_part = jnp.sum(back_wide * mixed_wide, axis=(0, 2)) / math.sqrt(data_size * seq_len)
    got_mixed, got_back = (
        lax.all_to_all(
            mixed_in.reshape(context_size, per_device, tok_rows),
            "ctx",
            split_axis=0,
            concat_axis=2,
            tiled=True,
        ),
        lax.all_to_all(
            back_grad.reshape(context_size, per_device, tok_rows),
            "ctx",
            split_axis=0,
            concat_axis=2,
            tiled=True,
        ),
    )
    mine = lax.dynamic_slice_in_dim(channel_group, context_index * per_device, per_device)
    membership = (mine[:, None] == jnp.arange(groups)[None, :]).astype(jnp.float32)
    positions = jnp.arange(seq_len).astype(jnp.float32) / seq_len
    plan = dft_plan(2 * seq_len)
    residue_mine = jnp.dot(membership, residue, precision=lax.Precision.HIGHEST)
    decay_mine = jnp.dot(membership, decay, precision=lax.Precision.HIGHEST)
    own_filter = contract(
        "cm,cmt->ct", residue_mine, jnp.exp(-decay_mine[:, :, None] * positions[None, None, :])
    )
    stacked = jnp.stack(
        [got_mixed[0].astype(jnp.float32), got_back[0].astype(jnp.float32), own_filter]
    )
    spec_real, spec_imag = forward_real(stacked, plan)
    mix_re, back_re, filt_re = (spec_real[0], spec_real[1], spec_real[2])
    mix_im, back_im, filt_im = (spec_imag[0], spec_imag[1], spec_imag[2])
    prod_real = jnp.stack(
        [
            filt_re * mix_re - filt_im * mix_im,
            filt_re * back_re + filt_im * back_im,
            mix_re * back_re + mix_im * back_im,
        ]
    )
    prod_imag = jnp.stack(
        [
            filt_re * mix_im + filt_im * mix_re,
            filt_re * back_im - filt_im * back_re,
            mix_re * back_im - mix_im * back_re,
        ]
    )
    results = inverse_real(prod_real, prod_imag, plan, 2 * seq_len)
    conv_state = results[0].astype(jnp.bfloat16)
    conv_back = results[1].astype(jnp.bfloat16)
    lagged = results[2]
    state_rows, back_rows = (
        lax.all_to_all(conv_state[None], "ctx", split_axis=2, concat_axis=0, tiled=True),
        lax.all_to_all(conv_back[None], "ctx", split_axis=2, concat_axis=0, tiled=True),
    )
    state_rows = state_rows.reshape(1, channels, tok_rows)
    back_rows = back_rows.reshape(1, channels, tok_rows)
    mixture = state_rows.astype(jnp.float32) + skip_bias[None, :, None] * mixed_wide
    conv_out = (gate_out.astype(jnp.float32) * mixture).astype(jnp.bfloat16)
    grad_gate_out = (cotangent.astype(jnp.float32) * mixture).astype(jnp.bfloat16)
    grad_mixed = back_rows.astype(jnp.float32) + skip_bias[None, :, None] * back_wide
    grad_gate_in = (grad_mixed * signal.astype(jnp.float32)).astype(jnp.bfloat16)
    grad_signal = (grad_mixed * gate_in.astype(jnp.float32)).astype(jnp.bfloat16)
    filter_part = jnp.dot(membership.T, lagged, precision=lax.Precision.HIGHEST) / math.sqrt(
        data_size * seq_len * GROUP_SIZE
    )
    summed_seqs = lax.psum(filter_part, "dp")
    grad_filter = lax.psum_scatter(summed_seqs, "ctx", scatter_dimension=1, tiled=True)
    grad_bias = lax.psum(bias_part, ("dp", "ctx"))
    block_steps = (context_index * tok_rows + jnp.arange(tok_rows)).astype(jnp.float32) / seq_len
    basis_local = jnp.exp(-decay[:, :, None] * block_steps[None, None, :])
    residue_local = contract("gt,gmt->gm", grad_filter, basis_local) / math.sqrt(seq_len)
    grad_residue = lax.psum(residue_local, "ctx")
    return (
        conv_out,
        grad_gate_out,
        grad_gate_in,
        grad_signal,
        grad_filter,
        grad_residue,
        grad_bias,
    )


def solution(mesh):
    return jax.shard_map(
        body,
        mesh=mesh,
        in_specs=(
            P("dp", None, "ctx"),
            P("dp", None, "ctx"),
            P("dp", None, "ctx"),
            P("dp", None, "ctx"),
            P(),
            P(),
            P(),
            P(),
        ),
        out_specs=(
            P("dp", None, "ctx"),
            P("dp", None, "ctx"),
            P("dp", None, "ctx"),
            P("dp", None, "ctx"),
            P(None, "ctx"),
            P(),
            P(),
        ),
        check_vma=False,
    )
```

profile of v0, /device:TPU:1, one launch (start us, length us, event | category | flops | bytes accessed | tf_op | source)
XLA Modules:
  0.0 446.4 jit_solution(15845458744475877318)
XLA Ops:
  7.2 1.9 fusion.51
  9.1 10.2 %all-to-all-start.1 = ((bf16[16,32,128]{2,1,0:T(8,128)(2,1)}), bf16[16,32,128]{2,1,0:T(8,128)(2,1)S(1)}, u32[]{:S(2)}, u32[]{:S(2)}) async-start(bf16[16,32,128]{2,1,0:T(8,128)(2,1)} %bitcast.6), calls=%async_computation.1 | async-start | bytes 262144 | tf_op jit(solution)/shard_map/all_to_all | solution.py:95
  19.3 0.8 dynamic_slice.3
  20.0 0.2 fusion.91
  20.2 0.9 convolution_negate_fusion.1
  21.2 2.6 fusion
  23.9 0.1 copy.48
  24.1 108.2 %psum.23 = f32[512]{0:T(512)} all-reduce(f32[512]{0:T(512)S(1)} %broadcast_multiply_fusion), channel_id=1, replica_groups=mesh['dp'=32,'ctx'=16] {'dp','ctx'}, use_global_device_ids=true, to_apply=%region_4.5 | all-reduce | flops 512 | bytes 4096 | tf_op jit(solution)/shard_map/psum | solution.py:153
  132.3 0.1 fusion.100
  132.4 4.3 all-to-all-start
  136.8 7.5 %all-to-all-done = bf16[16,32,128]{2,1,0:T(8,128)(2,1)S(1)} async-done(((bf16[16,32,128]{2,1,0:T(8,128)(2,1)}), bf16[16,32,128]{2,1,0:T(8,128)(2,1)S(1)}, u32[]{:S(2)}, u32[]{:S(2)}) %all-to-all-start) | async-done | bytes 131104 | tf_op jit(solution)/shard_map/all_to_all | solution.py:88
  144.3 1.5 fusion.42
  145.8 1.5 convolution_negate_fusion
  147.3 1.7 fusion.5
  149.0 1.7 fusion.7
  150.6 1.7 fusion.24
  152.3 1.7 fusion.21
  154.0 0.4 multiply_add_fusion.1
  154.4 0.4 multiply_subtract_fusion.3
  154.8 1.7 fusion.37
  156.5 1.8 fusion.36
  158.3 1.7 convolution_subtract_fusion
  160.0 1.6 convolution_add_fusion
  161.7 1.1 fusion.13
  162.7 1.1 fusion.146
  163.9 0.7 copy.28
  164.7 0.5 broadcast.137
  165.2 11.5 %reduce = bf16[2048,32]{1,0:T(8,128)(2,1)S(1)} reduce(bf16[2048,1,32]{2,1,0:T(2,128)(2,1)S(1)} %bitcast.118, bf16[]{:T(256)} %broadcast.137), dimensions={1}, to_apply=%bitcast.105.reduce_sub_computation | reduce | bytes 262146
  176.7 1.2 reshape.151
  177.9 4.0 all-to-all-start.3
  182.0 1.0 copy.26
  183.0 11.5 %reduce.1 = bf16[2048,32]{1,0:T(8,128)(2,1)S(1)} reduce(bf16[2048,1,32]{2,1,0:T(2,128)(2,1)S(1)} %bitcast.119, bf16[]{:T(256)} %broadcast.137), dimensions={1}, to_apply=%bitcast.103.reduce_sub_computation | reduce | bytes 262146
  194.6 1.2 reshape.149
  195.8 1.1 convolution_multiply_fusion
  196.9 7.3 %all-to-all-start.2 = ((bf16[16,2,2048]{2,1,0:T(2,128)(2,1)}), bf16[16,2,2048]{2,1,0:T(2,128)(2,1)S(1)}, u32[]{:S(2)}, u32[]{:S(2)}) async-start(bf16[16,2,2048]{2,1,0:T(2,128)(2,1)} %reshape.149), calls=%async_computation.2 | async-start | bytes 262144 | tf_op jit(solution)/shard_map/all_to_all | solution.py:137
  204.2 0.7 reshape.152
  204.9 1.1 bitcast_convert_fusion
  206.0 5.8 %all-to-all-done.2 = bf16[16,2,2048]{2,1,0:T(2,128)(2,1)S(1)} async-done(((bf16[16,2,2048]{2,1,0:T(2,128)(2,1)}), bf16[16,2,2048]{2,1,0:T(2,128)(2,1)S(1)}, u32[]{:S(2)}, u32[]{:S(2)}) %all-to-all-start.2) | async-done | bytes 131104 | tf_op jit(solution)/shard_map/all_to_all | solution.py:137
  211.8 0.7 reshape.150
  212.5 1.1 bitcast_convert_fusion.1
  213.7 0.3 copy.29
  214.0 0.3 copy.27
  214.3 0.2 copy-done.1
  214.8 2.0 fusion.44
  216.8 63.0 %reduce-scatter.2.cloned.1.call-done = f32[32,128]{1,0:T(8,128)} async-done(((f32[32,2048]{1,0:T(8,128)}), f32[32,128]{1,0:T(8,128)}) %reduce-scatter.2.cloned.1.call-update) | async-done | bytes 16400 | tf_op jit(solution)/shard_map/reduce_scatter | solution.py:152
  279.8 94.6 %psum.24 = f32[32,128]{1,0:T(8,128)S(1)} all-reduce(f32[32,128]{1,0:T(8,128)} %reduce-scatter.2.cloned.1.call-done), channel_id=1, replica_groups=mesh['dp'=32,'ctx'=16] {'dp'}, use_global_device_ids=true, to_apply=%region_0.0 | all-reduce | flops 4096 | bytes 32768 | tf_op jit(solution)/shard_map/psum | solution.py:151
  374.4 0.6 fusion.54
  375.1 64.0 %psum.22 = f32[32,16]{0,1:T(8,128)} all-reduce(f32[32,16]{0,1:T(8,128)S(1)} %bitcast_multiply_fusion), channel_id=1, replica_groups=mesh['dp'=32,'ctx'=16] {'ctx'}, use_global_device_ids=true, to_apply=%region_2.3 | all-reduce | flops 512 | bytes 4096 | tf_op jit(solution)/shard_map/psum | solution.py:157
  (35 shorter events, 0.9 us)
Async XLA Ops:
  7.2 12.9 %copy-start = (f32[32,16]{0,1:T(8,128)S(1)}, f32[32,16]{0,1:T(8,128)}, u32[]{:S(2)}) copy-start(f32[32,16]{0,1:T(8,128)} %param.12) | copy-start | bytes 6148
  7.2 16.7 %copy-start.6 = (f32[32,16]{0,1:T(8,128)S(1)}, f32[32,16]{0,1:T(8,128)}, u32[]{:S(2)}) copy-start(f32[32,16]{0,1:T(8,128)} %param.13) | copy-start | bytes 6148
  9.1 123.3 %all-to-all-start.1 = ((bf16[16,32,128]{2,1,0:T(8,128)(2,1)}), bf16[16,32,128]{2,1,0:T(8,128)(2,1)S(1)}, u32[]{:S(2)}, u32[]{:S(2)}) async-start(bf16[16,32,128]{2,1,0:T(8,128)(2,1)} %bitcast.6), calls=%async_computation.1 | async-start | bytes 262144 | tf_op jit(solution)/shard_map/all_to_all | solution.py:95
  132.4 11.9 %all-to-all-start = ((bf16[16,32,128]{2,1,0:T(8,128)(2,1)}), bf16[16,32,128]{2,1,0:T(8,128)(2,1)S(1)}, u32[]{:S(2)}, u32[]{:S(2)}) async-start(bf16[16,32,128]{2,1,0:T(8,128)(2,1)} %bitcast.3), calls=%async_computation | async-start | bytes 262144 | tf_op jit(solution)/shard_map/all_to_all | solution.py:88
  177.9 19.0 %all-to-all-start.3 = ((bf16[16,2,2048]{2,1,0:T(2,128)(2,1)}), bf16[16,2,2048]{2,1,0:T(2,128)(2,1)S(1)}, u32[]{:S(2)}, u32[]{:S(2)}) async-start(bf16[16,2,2048]{2,1,0:T(2,128)(2,1)} %reshape.151), calls=%async_computation.3 | async-start | bytes 262144 | tf_op jit(solution)/shard_map/all_to_all | solution.py:138
  181.9 97.9 %reduce-scatter.2.cloned.1.call-start = ((), (), s32[]{:S(2)}) async-start(), calls=%async_computation.5 | async-start | bytes 278528 | tf_op jit(solution)/shard_map/reduce_scatter | solution.py:152
  196.9 14.9 %all-to-all-start.2 = ((bf16[16,2,2048]{2,1,0:T(2,128)(2,1)}), bf16[16,2,2048]{2,1,0:T(2,128)(2,1)S(1)}, u32[]{:S(2)}, u32[]{:S(2)}) async-start(bf16[16,2,2048]{2,1,0:T(2,128)(2,1)} %reshape.149), calls=%async_computation.2 | async-start | bytes 262144 | tf_op jit(solution)/shard_map/all_to_all | solution.py:137
  213.7 0.9 copy-start.1
  213.7 1.0 copy-start.2
  213.7 1.0 copy-start.3
  213.7 1.1 copy-start.4
  213.7 1.1 copy-start.7
  374.4 64.7 %copy-start.5 = (f32[32,128]{1,0:T(8,128)}, f32[32,128]{1,0:T(8,128)S(1)}, u32[]{:S(2)}) copy-start(f32[32,128]{1,0:T(8,128)S(1)} %psum.24) | copy-start | bytes 49156
Sparse Core Ops, SparseCore 0:
  197.0 82.7 reduce-scatter.1
where the time goes:
time: 451 us; the launch traced here: 446 us
  blocking collectives  267 us (59%)
  waiting for transfers between devices  76.4 us (17%)
  other arithmetic  30.2 us (7%)
  starting transfers between devices  25.8 us (6%)
  matrix products  24 us (5%)
  between operations  14.8 us (3%)
  local copies, waits for them, and re-layouts  8.33 us (2%)
    psum x1, blocking collectives, body(): grad_bias = lax.psum(bias_part, ('dp', 'ctx'))  108 us
    psum x1, blocking collectives, body(): summed_seqs = lax.psum(filter_part, 'dp')  94.6 us
    psum x1, blocking collectives, body(): grad_residue = lax.psum(residue_local, 'ctx')  64 us
    reduce_scatter x1, waiting for transfers between devices, body(): lax.psum_scatter(summed_seqs, 'ctx', scatter_dimension=1, tiled=True)  63 us
    unnamed x2, other arithmetic  23.1 us
    dot_general x14, matrix products, contract(): return jnp.einsum(form, left, right, precision=lax.Precision.HIGHEST)  21.8 us
    all_to_all x1, starting transfers between devices, body(): lax.all_to_all(back_grad.reshape(context_size, per_device, tok_rows), 'ct...  10.2 us
  transfers between devices with their start and end apart: 5, of which 3 were waited for; matrix products, arithmetic and copies ran while one was open for 6% of the time, Pallas kernels for 0%

commit v1 on v0

v1 whole, which is shorter than its diff:
```python
import functools
import math

import jax
import jax.numpy as jnp
from jax import lax
from jax.experimental import pallas as pl
from jax.experimental.pallas import tpu as pltpu
from jax.sharding import PartitionSpec as P

GROUP_SIZE = 16
MESH = pl.DeviceIdType.MESH
EXACT = lax.Precision.HIGHEST
F32 = jnp.float32
BF16 = jnp.bfloat16


def iota(shape, dim):
    return lax.broadcasted_iota(jnp.int32, shape, dim)


def matmul(left, right, dims=(1, 0), precision=None):
    return lax.dot_general(
        left,
        right,
        (((dims[0],), (dims[1],)), ((), ())),
        precision=precision,
        preferred_element_type=F32,
    )


def kernel(
    data_size,
    ctx_size,
    gate_out,
    gate_in,
    signal,
    cotangent,
    residue,
    decay,
    skip_bias,
    channel_group,
    conv_out,
    grad_gate_out,
    grad_gate_in,
    grad_signal,
    grad_filter,
    grad_residue,
    grad_bias,
    sorted_in,
    got,
    unsort,
    bias_wide,
    ranks,
    basis,
    taps,
    lags,
    corr_send,
    corr_got,
    back_send,
    back_got,
    sum_got,
    sum_send,
    all_got,
    final,
    send_sems,
    recv_sems,
):
    groups = residue.shape[0]
    channels, rows = gate_out.shape
    seq_len = rows * ctx_size
    own = channels // ctx_size
    own_groups = own // GROUP_SIZE
    share = groups // data_size
    data_index = lax.axis_index("dp")
    ctx_index = lax.axis_index("ctx")

    def over_ctx(step):
        lax.fori_loop(1, ctx_size, lambda o, c: (step(lax.rem(ctx_index + o, ctx_size)), c)[1], 0)

    def over_data(step):
        lax.fori_loop(1, data_size, lambda o, c: (step(lax.rem(data_index + o, data_size)), c)[1], 0)

    def push(src, dst, phase, target):
        pltpu.make_async_remote_copy(
            src_ref=src,
            dst_ref=dst,
            send_sem=send_sems.at[phase],
            recv_sem=recv_sems.at[phase],
            device_id=target,
            device_id_type=MESH,
        ).start()

    def arrived(span, phase):
        pltpu.make_async_copy(span, span, recv_sems.at[phase]).wait()

    def sent(span, phase):
        pltpu.make_async_copy(span, span, send_sems.at[phase]).wait()

    barrier = pltpu.get_barrier_semaphore()
    over_ctx(
        lambda t: pl.semaphore_signal(barrier, inc=1, device_id={"ctx": t}, device_id_type=MESH)
    )
    over_data(
        lambda t: pl.semaphore_signal(barrier, inc=1, device_id={"dp": t}, device_id_type=MESH)
    )

    member = iota((groups, channels), 0) == channel_group[...]
    before = jnp.where(iota((channels, channels), 0) < iota((channels, channels), 1), 1.0, 0.0)
    rank = matmul(jnp.where(member, 1.0, 0.0).astype(BF16), before.astype(BF16))
    rank = jnp.sum(jnp.where(member, rank, 0.0), axis=0, keepdims=True)
    ranks[...] = rank
    first = jnp.sum(
        jnp.where(member, iota((groups, channels), 0).astype(F32), 0.0), axis=0, keepdims=True
    )
    place = first * GROUP_SIZE + rank
    sort = jnp.where(iota((channels, channels), 0).astype(F32) == place, 1.0, 0.0).astype(BF16)

    mixed = (gate_in[...].astype(F32) * signal[...].astype(F32)).astype(BF16)
    back = (cotangent[...].astype(F32) * gate_out[...].astype(F32)).astype(BF16)
    sorted_in[...] = matmul(sort, jnp.concatenate([mixed, back], axis=1)).astype(BF16)
    got[ctx_index] = sorted_in[pl.ds(pl.multiple_of(ctx_index * own, own), own)]

    pl.semaphore_wait(barrier, ctx_size - 1 + data_size - 1)
    over_ctx(
        lambda t: push(
            sorted_in.at[pl.ds(pl.multiple_of(t * own, own), own)],
            got.at[ctx_index],
            0,
            {"ctx": t},
        )
    )

    place_wide = jnp.transpose(jnp.broadcast_to(place, (128, channels)))
    unsort[...] = jnp.where(
        iota((channels, channels), 1).astype(F32) == place_wide[:, :1], 1.0, 0.0
    ).astype(BF16)
    bias_wide[...] = jnp.transpose(jnp.broadcast_to(skip_bias[...], (rows, channels)))
    modes = residue.shape[1]
    lane = iota((modes, rows), 1).astype(F32)
    for g in range(own_groups):
        pick = jnp.where(iota((groups, rows), 0) == ctx_index * own_groups + g, 1.0, 0.0)
        rate = matmul(decay[...], pick, (0, 0), EXACT)
        weight = matmul(residue[...], pick, (0, 0), EXACT)
        for i in range(ctx_size):
            basis[g, :, i * rows : (i + 1) * rows] = jnp.exp(-rate * ((lane + i * rows) / seq_len))
        filt = matmul(weight * jnp.exp(rate * (lane / seq_len)), basis[g], (0, 0), EXACT)
        causal = iota((rows, rows), 1) >= iota((rows, rows), 0)
        taps[g, :, :rows] = jnp.zeros((rows, rows), BF16)
        taps[g, :, rows : 2 * rows] = jnp.where(causal, filt[:, :rows], 0.0).astype(BF16)
        taps[g, :, 2 * rows :] = filt[:, rows:].astype(BF16)

    arrived(got.at[pl.ds(0, ctx_size - 1)], 0)

    for g in range(own_groups):
        mine = slice(g * GROUP_SIZE, (g + 1) * GROUP_SIZE)
        blocks = ctx_size * GROUP_SIZE
        mix = got[:, mine, :rows].reshape(blocks, rows)
        grad = got[:, mine, rows:].reshape(blocks, rows)
        mix_t = jnp.transpose(mix)

        def shifted(k):
            if k == 0:
                return grad
            return jnp.concatenate(
                [grad[k * GROUP_SIZE :], jnp.zeros((k * GROUP_SIZE, rows), BF16)], axis=0
            )

        for k in range(0, ctx_size, 2):
            pair = jnp.concatenate([shifted(k), shifted(k + 1)], axis=1)
            lags[:, k * rows : (k + 2) * rows] = matmul(mix_t, pair)
        lags[:, seq_len:] = jnp.zeros((rows, rows), F32)
        width = seq_len + rows
        parts = [lags[a * 8 : (a + 1) * 8, :] for a in range(rows // 8)]
        shift = 8
        while len(parts) > 1:
            parts = [
                parts[a] + pltpu.roll(parts[a + 1], width - shift, 1)
                for a in range(0, len(parts), 2)
            ]
            shift *= 2
        skew = parts[0]
        row = iota((8, width), 0)
        for bit in (1, 2, 4):
            skew = jnp.where(row & bit != 0, pltpu.roll(skew, width - bit, 1), skew)
        corr = jnp.sum(skew, axis=0, keepdims=True)
        modal = jnp.zeros((modes, rows), F32)
        for i in range(ctx_size):
            span = slice(i * rows, (i + 1) * rows)
            modal = modal + basis[g, :, span] * corr[:, span]
            corr_send[i, g, :, :rows] = corr[:, span]
        direct = jnp.zeros((GROUP_SIZE, rows), F32)
        for i in range(ctx_size):
            direct = direct + got[i, mine, :rows].astype(F32) * got[i, mine, rows:].astype(F32)
        stack = jnp.concatenate(
            [modal, direct, jnp.zeros((rows - modes - GROUP_SIZE, rows), F32)], axis=0
        )
        small = matmul(jnp.ones((8, rows), F32), stack, (1, 1), EXACT)[:1]
        for i in range(ctx_size):
            corr_send[i, g, :, rows:] = small
    for g in range(own_groups):
        corr_got[ctx_index * own_groups + g] = corr_send[ctx_index, g]
    over_ctx(
        lambda t: push(
            corr_send.at[t],
            corr_got.at[pl.ds(ctx_index * own_groups, own_groups)],
            1,
            {"ctx": t},
        )
    )

    pairs = ctx_size // 2
    for g in range(own_groups):
        mine = slice(g * GROUP_SIZE, (g + 1) * GROUP_SIZE)
        wide = [
            jnp.concatenate([got[2 * p, mine, :], got[2 * p + 1, mine, :]], axis=1)
            for p in range(pairs)
        ]
        wide = jnp.concatenate(wide, axis=0)
        mix = jnp.concatenate([wide[:, :rows], wide[:, 2 * rows : 3 * rows]], axis=1)
        grad = jnp.concatenate([wide[:, rows : 2 * rows], wide[:, 3 * rows :]], axis=1)
        state = jnp.zeros((pairs * GROUP_SIZE, 2 * rows), F32)
        prior = jnp.zeros((pairs * GROUP_SIZE, 2 * rows), F32)
        for q in range(pairs):
            block = jnp.concatenate(
                [
                    taps[g, :, (2 * q + 1) * rows : (2 * q + 3) * rows],
                    taps[g, :, 2 * q * rows : (2 * q + 2) * rows],
                ],
                axis=0,
            )
            cut = q * GROUP_SIZE
            left = pairs * GROUP_SIZE - cut
            ahead = matmul(mix[:left], block)
            behind = matmul(grad[cut:], block, (1, 1))
            if q == 0:
                state, prior = ahead, behind
            else:
                gap = jnp.zeros((cut, 2 * rows), F32)
                state = state + jnp.concatenate([gap, ahead], axis=0)
                prior = prior + jnp.concatenate([behind, gap], axis=0)
        state = state.astype(BF16)
        prior = prior.astype(BF16)
        for i in range(ctx_size):
            at = slice((i // 2) * GROUP_SIZE, (i // 2 + 1) * GROUP_SIZE)
            span = slice((i % 2) * rows, (i % 2 + 1) * rows)
            back_send[i, mine, :rows] = state[at, span]
            back_send[i, mine, rows:] = prior[at, span]
    back_got[pl.ds(pl.multiple_of(ctx_index * own, own), own)] = back_send[ctx_index]
    over_ctx(
        lambda t: push(
            back_send.at[t],
            back_got.at[pl.ds(pl.multiple_of(ctx_index * own, own), own)],
            2,
            {"ctx": t},
        )
    )

    arrived(corr_got.at[pl.ds(0, own_groups * (ctx_size - 1))], 1)
    sum_got[data_index] = corr_got[pl.ds(data_index * share, share)]
    over_data(
        lambda t: push(
            corr_got.at[pl.ds(t * share, share)], sum_got.at[data_index], 3, {"dp": t}
        )
    )

    arrived(back_got.at[pl.ds(0, own * (ctx_size - 1))], 2)
    results = matmul(unsort[...], back_got[...])
    wide_gate = gate_out[...].astype(F32)
    wide_cot = cotangent[...].astype(F32)
    wide_in = gate_in[...].astype(F32)
    wide_signal = signal[...].astype(F32)
    mixed_wide = (wide_in * wide_signal).astype(BF16).astype(F32)
    back_wide = (wide_cot * wide_gate).astype(BF16).astype(F32)
    mixture = results[:, :rows] + bias_wide[...] * mixed_wide
    conv_out[...] = (wide_gate * mixture).astype(BF16)
    grad_gate_out[...] = (wide_cot * mixture).astype(BF16)
    grad_mixed = results[:, rows:] + bias_wide[...] * back_wide
    grad_gate_in[...] = (grad_mixed * wide_signal).astype(BF16)
    grad_signal[...] = (grad_mixed * wide_in).astype(BF16)

    arrived(sum_got.at[pl.ds(0, data_size - 1)], 3)
    total = sum_got[0]
    for i in range(1, data_size):
        total = total + sum_got[i]
    at = iota((1, 1, 2 * rows), 2)
    filter_scale = 1.0 / math.sqrt(data_size * seq_len * GROUP_SIZE)
    scale = jnp.where(
        at < rows,
        filter_scale,
        jnp.where(
            at < rows + modes,
            filter_scale / math.sqrt(seq_len),
            1.0 / math.sqrt(data_size * seq_len),
        ),
    )
    sum_send[...] = total * scale
    all_got[pl.ds(data_index * share, share)] = sum_send[...]
    over_data(
        lambda t: push(sum_send, all_got.at[pl.ds(data_index * share, share)], 4, {"dp": t})
    )
    arrived(all_got.at[pl.ds(0, share * (data_size - 1))], 4)
    for g in range(groups):
        final[g : g + 1, :] = all_got[g]
    grad_filter[...] = final[:, :rows]
    small = final[:, rows:]
    grad_residue[...] = small[:, :modes]
    spread = matmul(small, jnp.where(member, 1.0, 0.0), (0, 0), EXACT)
    hit = iota((rows, channels), 0).astype(F32) == ranks[...] + modes
    grad_bias[...] = jnp.sum(jnp.where(hit, spread, 0.0), axis=0, keepdims=True)

    sent(got.at[pl.ds(0, ctx_size - 1)], 0)
    sent(corr_got.at[pl.ds(0, own_groups * (ctx_size - 1))], 1)
    sent(back_got.at[pl.ds(0, own * (ctx_size - 1))], 2)
    sent(sum_got.at[pl.ds(0, data_size - 1)], 3)
    sent(all_got.at[pl.ds(0, share * (data_size - 1))], 4)


def body(gate_out, gate_in, signal, cotangent, residue, decay, skip_bias, channel_group):
    data_size = lax.axis_size("dp")
    ctx_size = lax.axis_size("ctx")
    _, channels, rows = gate_out.shape
    groups, modes = residue.shape
    own = channels // ctx_size
    own_groups = own // GROUP_SIZE
    share = groups // data_size
    seq_len = rows * ctx_size
    vmem = pl.BlockSpec(memory_space=pltpu.VMEM)
    wide = jax.ShapeDtypeStruct((channels, rows), BF16)
    flat = lambda a: a.reshape(channels, rows)
    results = pl.pallas_call(
        functools.partial(kernel, data_size, ctx_size),
        out_shape=[
            wide,
            wide,
            wide,
            wide,
            jax.ShapeDtypeStruct((groups, rows), F32),
            jax.ShapeDtypeStruct((groups, modes), F32),
            jax.ShapeDtypeStruct((1, channels), F32),
        ],
        in_specs=[vmem] * 8,
        out_specs=[vmem] * 7,
        scratch_shapes=[
            pltpu.VMEM((channels, 2 * rows), BF16),
            pltpu.VMEM((ctx_size, own, 2 * rows), BF16),
            pltpu.VMEM((channels, channels), BF16),
            pltpu.VMEM((channels, rows), F32),
            pltpu.VMEM((1, channels), F32),
            pltpu.VMEM((own_groups, modes, seq_len), F32),
            pltpu.VMEM((own_groups, rows, seq_len + rows), BF16),
            pltpu.VMEM((rows, seq_len + rows), F32),
            pltpu.VMEM((ctx_size, own_groups, 1, 2 * rows), F32),
            pltpu.VMEM((groups, 1, 2 * rows), F32),
            pltpu.VMEM((ctx_size, own, 2 * rows), BF16),
            pltpu.VMEM((channels, 2 * rows), BF16),
            pltpu.VMEM((data_size, share, 1, 2 * rows), F32),
            pltpu.VMEM((share, 1, 2 * rows), F32),
            pltpu.VMEM((groups, 1, 2 * rows), F32),
            pltpu.VMEM((groups, 2 * rows), F32),
            pltpu.SemaphoreType.DMA((5,)),
            pltpu.SemaphoreType.DMA((5,)),
        ],
        compiler_params=pltpu.CompilerParams(
            collective_id=0, has_side_effects=True, vmem_limit_bytes=32 * 1024 * 1024
        ),
        cost_estimate=pl.CostEstimate(
            flops=2 * 400_000_000, bytes_accessed=2_000_000, transcendentals=100_000
        ),
    )(
        flat(gate_out),
        flat(gate_in),
        flat(signal),
        flat(cotangent),
        residue,
        decay,
        skip_bias.reshape(1, channels),
        channel_group.reshape(1, channels),
    )
    lifted = tuple(a.reshape(1, channels, rows) for a in results[:4])
    return lifted + (results[4], results[5], results[6].reshape(channels))


def solution(mesh):
    return jax.shard_map(
        body,
        mesh=mesh,
        in_specs=(
            P("dp", None, "ctx"),
            P("dp", None, "ctx"),
            P("dp", None, "ctx"),
            P("dp", None, "ctx"),
            P(),
            P(),
            P(),
            P(),
        ),
        out_specs=(
            P("dp", None, "ctx"),
            P("dp", None, "ctx"),
            P("dp", None, "ctx"),
            P("dp", None, "ctx"),
            P(None, "ctx"),
            P(),
            P(),
        ),
        check_vma=False,
    )
```

time: 451 us -> 56.6 us (0.13)
  blocking collectives: 267 us -> 0 us
  waiting for transfers between devices: 76.4 us -> 0 us
  Pallas kernels: 0 us -> 44.8 us
  other arithmetic: 30.2 us -> 0 us
  starting transfers between devices: 25.8 us -> 0 us
  matrix products: 24 us -> 0 us
  between operations: 14.8 us -> 0.66 us
    psum x3 -> x0, blocking collectives: 267 us -> none  [the longest x1 108 us: body(): grad_bias = lax.psum(bias_part, ('dp', 'ctx'))]
    reduce_scatter x1 -> x0, waiting for transfers between devices: 63 us -> none  [body(): lax.psum_scatter(summed_seqs, 'ctx', scatter_dimension=1, tiled=True)]
    pallas_call x0 -> x1, Pallas kernels: none -> 44.8 us  [body(): pl.pallas_call(functools.partial(kernel, data_size, ctx_size), out_shape=...]
    all_to_all x4 -> x0, starting transfers between devices: 25.8 us -> none  [the longest x1 10.2 us: body(): lax.all_to_all(back_grad.reshape(context_size, per_device, tok_rows), 'ct...]
    dot_general x17 -> x0, matrix products: 24 us -> none  [the longest x14 21.8 us: contract(): return jnp.einsum(form, left, right, precision=lax.Precision.HIGHEST)]
    unnamed x2 -> x0, other arithmetic: 23.1 us -> none
    all_to_all x4 -> x0, waiting for transfers between devices: 13.4 us -> none  [the longest x1 7.52 us: body(): lax.all_to_all(mixed_in.reshape(context_size, per_device, tok_rows), 'ctx...]
    unnamed x22 -> x25, local copies, waits for them, and re-layouts: 4.78 us -> 10.2 us
  transfers between devices with their start and end apart: 5 -> 0, of which waited for: 3 -> 0; matrix products, arithmetic and copies ran while one was open for 6% -> 0% of each run, Pallas kernels for 0% -> 0%
where the time goes in v1:
time: 56.6 us; the launch traced here: 55.6 us
  Pallas kernels  44.8 us (79%)
  local copies, waits for them, and re-layouts  10.2 us (18%)
  between operations  0.66 us (1%)
    pallas_call x1, Pallas kernels, body(): pl.pallas_call(functools.partial(kernel, data_size, ctx_size), out_shape=...  44.8 us
    unnamed x25, local copies, waits for them, and re-layouts  10.2 us

profile of v1, /device:TPU:1, one launch (start us, length us, event | category | flops | bytes accessed | tf_op | source)
XLA Modules:
  0.0 55.6 jit_solution(4166217284394750521)
XLA Ops:
  0.6 0.0 copy-start.6
  0.6 0.7 %copy-done.6 = f32[32,16]{0,1:T(8,128)S(1)} copy-done((f32[32,16]{0,1:T(8,128)S(1)}, f32[32,16]{0,1:T(8,128)}, u32[]{:S(2)}) %copy-start.6) | copy-done | bytes 2072
  1.3 0.0 copy-start.7
  1.3 0.1 copy.15.residue
  1.4 0.6 %copy-done.7 = f32[32,16]{0,1:T(8,128)S(1)} copy-done((f32[32,16]{0,1:T(8,128)S(1)}, f32[32,16]{0,1:T(8,128)}, u32[]{:S(2)}) %copy-start.7) | copy-done | bytes 2072
  2.0 0.0 copy-start.4
  2.0 0.0 copy-start.5
  2.0 0.1 copy.16.decay
  2.1 0.6 %copy-done.4 = f32[512]{0:T(512)S(1)} copy-done((f32[512]{0:T(512)S(1)}, f32[512]{0:T(512)}, u32[]{:S(2)}) %copy-start.4) | copy-done | bytes 2072
  2.7 0.0 copy-done.5
  2.7 0.0 copy-start
  2.7 0.9 %copy-done = bf16[1,512,128]{2,1,0:T(8,128)(2,1)S(1)} copy-done((bf16[1,512,128]{2,1,0:T(8,128)(2,1)S(1)}, bf16[1,512,128]{2,1,0:T(8,128)(2,1)}, u32[]{:S(2)}) %copy-start) | copy-done | bytes 131096
  3.6 0.0 copy-start.1
  3.6 0.9 %copy-done.1 = bf16[1,512,128]{2,1,0:T(8,128)(2,1)S(1)} copy-done((bf16[1,512,128]{2,1,0:T(8,128)(2,1)S(1)}, bf16[1,512,128]{2,1,0:T(8,128)(2,1)}, u32[]{:S(2)}) %copy-start.1) | copy-done | bytes 131096
  4.5 0.0 copy-start.2
  4.5 0.9 %copy-done.2 = bf16[1,512,128]{2,1,0:T(8,128)(2,1)S(1)} copy-done((bf16[1,512,128]{2,1,0:T(8,128)(2,1)S(1)}, bf16[1,512,128]{2,1,0:T(8,128)(2,1)}, u32[]{:S(2)}) %copy-start.2) | copy-done | bytes 131096
  5.4 0.0 copy-start.3
  5.4 0.9 %copy-done.3 = bf16[1,512,128]{2,1,0:T(8,128)(2,1)S(1)} copy-done((bf16[1,512,128]{2,1,0:T(8,128)(2,1)S(1)}, bf16[1,512,128]{2,1,0:T(8,128)(2,1)}, u32[]{:S(2)}) %copy-start.3) | copy-done | bytes 131096
  6.3 44.8 %shard_map.135 = (bf16[512,128]{1,0:T(8,128)(2,1)S(1)}, bf16[512,128]{1,0:T(8,128)(2,1)S(1)}, bf16[512,128]{1,0:T(8,128)(2,1)S(1)}, bf16[512,128]{1,0:T(8,128)(2...) custom-call(bf16[512,128]{1,0:T(8,128)(2,1)S(1)} %bitcast.16, ...), custom_call_target="tpu_custom_call" | custom-call | flops 800000000 | bytes 2000000 | tf_op jit(solution)/shard_map/pallas_call | solution.py:331
  51.1 0.7 %copy.17 = f32[32,16]{0,1:T(8,128)} copy(f32[32,16]{1,0:T(8,128)S(1)} %get-tuple-element.26) | data formatting | bytes 4096
  51.8 0.7 %copy.24 = bf16[1,512,128]{2,1,0:T(8,128)(2,1)} copy(bf16[1,512,128]{2,1,0:T(8,128)(2,1)S(1)} %bitcast.14) | data formatting | bytes 262144
  52.5 0.7 %copy.25 = bf16[1,512,128]{2,1,0:T(8,128)(2,1)} copy(bf16[1,512,128]{2,1,0:T(8,128)(2,1)S(1)} %bitcast.13) | data formatting | bytes 262144
  53.1 0.7 %copy.26 = bf16[1,512,128]{2,1,0:T(8,128)(2,1)} copy(bf16[1,512,128]{2,1,0:T(8,128)(2,1)S(1)} %bitcast.12) | data formatting | bytes 262144
  53.8 0.7 %copy.27 = bf16[1,512,128]{2,1,0:T(8,128)(2,1)} copy(bf16[1,512,128]{2,1,0:T(8,128)(2,1)S(1)} %bitcast.11) | data formatting | bytes 262144
  54.4 0.6 %copy.28 = f32[32,128]{1,0:T(8,128)} copy(f32[32,128]{1,0:T(8,128)S(1)} %get-tuple-element.39) | data formatting | bytes 32768
  55.0 0.6 %copy.29 = f32[512]{0:T(512)} copy(f32[512]{0:T(512)S(1)} %bitcast.15) | data formatting | bytes 4096
Async XLA Ops:
  0.6 0.7 %copy-start.6 = (f32[32,16]{0,1:T(8,128)S(1)}, f32[32,16]{0,1:T(8,128)}, u32[]{:S(2)}) copy-start(f32[32,16]{0,1:T(8,128)} %param.12) | copy-start | bytes 6148
  1.3 0.7 %copy-start.7 = (f32[32,16]{0,1:T(8,128)S(1)}, f32[32,16]{0,1:T(8,128)}, u32[]{:S(2)}) copy-start(f32[32,16]{0,1:T(8,128)} %param.13) | copy-start | bytes 6148
  2.0 0.7 %copy-start.4 = (f32[512]{0:T(512)S(1)}, f32[512]{0:T(512)}, u32[]{:S(2)}) copy-start(f32[512]{0:T(512)} %param.14) | copy-start | bytes 6148
  2.0 0.7 %copy-start.5 = (s32[512]{0:T(512)S(1)}, s32[512]{0:T(512)}, u32[]{:S(2)}) copy-start(s32[512]{0:T(512)} %param.15) | copy-start | bytes 6148
  2.7 0.9 %copy-start = (bf16[1,512,128]{2,1,0:T(8,128)(2,1)S(1)}, bf16[1,512,128]{2,1,0:T(8,128)(2,1)}, u32[]{:S(2)}) copy-start(bf16[1,512,128]{2,1,0:T(8,128)(2,1)} %param.8) | copy-start | bytes 393220
  3.6 0.9 %copy-start.1 = (bf16[1,512,128]{2,1,0:T(8,128)(2,1)S(1)}, bf16[1,512,128]{2,1,0:T(8,128)(2,1)}, u32[]{:S(2)}) copy-start(bf16[1,512,128]{2,1,0:T(8,128)(2,1)} %param.9) | copy-start | bytes 393220
  4.5 0.9 %copy-start.2 = (bf16[1,512,128]{2,1,0:T(8,128)(2,1)S(1)}, bf16[1,512,128]{2,1,0:T(8,128)(2,1)}, u32[]{:S(2)}) copy-start(bf16[1,512,128]{2,1,0:T(8,128)(2,1)} %param.10) | copy-start | bytes 393220
  5.4 0.9 %copy-start.3 = (bf16[1,512,128]{2,1,0:T(8,128)(2,1)S(1)}, bf16[1,512,128]{2,1,0:T(8,128)(2,1)}, u32[]{:S(2)}) copy-start(bf16[1,512,128]{2,1,0:T(8,128)(2,1)} %param.11) | copy-start | bytes 393220

commit v2 on v1

v2 whole, which is shorter than its diff:
```python
import functools
import math

import jax
import jax.numpy as jnp
from jax import lax
from jax.experimental import pallas as pl
from jax.experimental.pallas import tpu as pltpu
from jax.sharding import PartitionSpec as P

GROUP_SIZE = 16
PLANE_SEQS = 2
MESH = pl.DeviceIdType.MESH
EXACT = lax.Precision.HIGHEST
F32 = jnp.float32
BF16 = jnp.bfloat16


def iota(shape, dim):
    return lax.broadcasted_iota(jnp.int32, shape, dim)


def matmul(left, right, dims=(1, 0), precision=None):
    return lax.dot_general(
        left,
        right,
        (((dims[0],), (dims[1],)), ((), ())),
        precision=precision,
        preferred_element_type=F32,
    )


def kernel(
    data_size,
    ctx_size,
    gate_out_hbm,
    gate_in_hbm,
    signal_hbm,
    cotangent_hbm,
    residue_hbm,
    decay_hbm,
    skip_bias_hbm,
    channel_group_hbm,
    conv_out_hbm,
    grad_gate_out_hbm,
    grad_gate_in_hbm,
    grad_signal_hbm,
    grad_filter_hbm,
    grad_residue_hbm,
    grad_bias_hbm,
    gate_out,
    gate_in,
    signal,
    cotangent,
    residue,
    decay,
    skip_bias,
    channel_group,
    load_sems,
    conv_out,
    grad_gate_out,
    grad_gate_in,
    grad_signal,
    grad_filter,
    grad_residue,
    grad_bias,
    store_sems,
    sorted_in,
    got,
    unsort,
    bias_wide,
    ranks,
    basis,
    taps,
    lags,
    term_send,
    term_got,
    back_send,
    back_got,
    sum_send,
    sum_got,
    final,
    send_sems,
    recv_sems,
):
    modes, groups = residue.shape
    channels, rows = gate_out.shape
    seq_len = rows * ctx_size
    depth = data_size // PLANE_SEQS
    blocks = ctx_size * GROUP_SIZE
    ctx_index = lax.axis_index("ctx")
    plane_seq = lax.axis_index("dp") // depth
    level = lax.axis_index("dp") % depth
    plane_index = plane_seq * ctx_size + ctx_index

    def over_plane(step):
        def one(o, c):
            peer = lax.rem(plane_index + o, groups)
            seq = peer // ctx_size
            rank = peer - seq * ctx_size
            step(peer, seq, rank, {"dp": seq * depth + level, "ctx": rank})
            return c

        lax.fori_loop(1, groups, one, 0)

    def over_column(step):
        def one(o, c):
            peer = lax.rem(level + o, depth)
            step({"dp": plane_seq * depth + peer})
            return c

        lax.fori_loop(1, depth, one, 0)

    def push(src, dst, phase, target):
        pltpu.make_async_remote_copy(
            src_ref=src,
            dst_ref=dst,
            send_sem=send_sems.at[phase],
            recv_sem=recv_sems.at[phase],
            device_id=target,
            device_id_type=MESH,
        ).start()

    def arrived(span, phase):
        pltpu.make_async_copy(span, span, recv_sems.at[phase]).wait()

    def sent(span, phase):
        pltpu.make_async_copy(span, span, send_sems.at[phase]).wait()

    def arrived_plane(phase):
        span = sorted_in.at[pl.ds(0, channels - GROUP_SIZE)]
        arrived(span, phase)

    loads = [
        pltpu.make_async_copy(src, dst, load_sems.at[i])
        for i, (src, dst) in enumerate(
            [
                (channel_group_hbm, channel_group),
                (gate_in_hbm, gate_in),
                (signal_hbm, signal),
                (gate_out_hbm, gate_out),
                (cotangent_hbm, cotangent),
                (decay_hbm, decay),
                (residue_hbm, residue),
                (skip_bias_hbm, skip_bias),
            ]
        )
    ]
    for load in loads:
        load.start()
    stores = [
        pltpu.make_async_copy(src, dst, store_sems.at[i])
        for i, (src, dst) in enumerate(
            [
                (conv_out, conv_out_hbm),
                (grad_gate_out, grad_gate_out_hbm),
                (grad_gate_in, grad_gate_in_hbm),
                (grad_signal, grad_signal_hbm),
                (grad_filter, grad_filter_hbm),
                (grad_residue, grad_residue_hbm),
                (grad_bias, grad_bias_hbm),
            ]
        )
    ]

    barrier = pltpu.get_barrier_semaphore()
    over_plane(
        lambda p, s, k, target: pl.semaphore_signal(
            barrier, inc=1, device_id=target, device_id_type=MESH
        )
    )
    over_column(
        lambda target: pl.semaphore_signal(barrier, inc=1, device_id=target, device_id_type=MESH)
    )

    loads[0].wait()
    member = iota((groups, channels), 0) == channel_group[...]
    before = jnp.where(iota((channels, channels), 0) < iota((channels, channels), 1), 1.0, 0.0)
    rank = matmul(jnp.where(member, 1.0, 0.0).astype(BF16), before.astype(BF16))
    rank = jnp.sum(jnp.where(member, rank, 0.0), axis=0, keepdims=True)
    ranks[...] = rank
    first = jnp.sum(
        jnp.where(member, iota((groups, channels), 0).astype(F32), 0.0), axis=0, keepdims=True
    )
    place = first * GROUP_SIZE + rank
    sort = jnp.where(iota((channels, channels), 0).astype(F32) == place, 1.0, 0.0).astype(BF16)

    for load in loads[1:5]:
        load.wait()
    mixed = (gate_in[...].astype(F32) * signal[...].astype(F32)).astype(BF16)
    back = (cotangent[...].astype(F32) * gate_out[...].astype(F32)).astype(BF16)
    sorted_in[...] = matmul(sort, jnp.concatenate([mixed, back], axis=1)).astype(BF16)

    def channels_of(peer):
        return pl.ds(pl.multiple_of(peer * GROUP_SIZE, GROUP_SIZE), GROUP_SIZE)

    got[plane_seq, ctx_index] = sorted_in[channels_of(plane_index)]

    pl.semaphore_wait(barrier, groups - 1 + depth - 1)
    over_plane(
        lambda p, s, k, target: push(
            sorted_in.at[channels_of(p)], got.at[plane_seq, ctx_index], 0, target
        )
    )

    for load in loads[5:]:
        load.wait()
    place_wide = jnp.transpose(jnp.broadcast_to(place, (128, channels)))
    unsort[...] = jnp.where(
        iota((channels, channels), 1).astype(F32) == place_wide[:, :1], 1.0, 0.0
    ).astype(BF16)
    bias_wide[...] = jnp.transpose(jnp.broadcast_to(skip_bias[...], (rows, channels)))
    lane = iota((modes, rows), 1).astype(F32)
    pick = jnp.where(iota((groups, rows), 0) == plane_index, 1.0, 0.0)
    rate = matmul(decay[...], pick, precision=EXACT)
    weight = matmul(residue[...], pick, precision=EXACT)
    for i in range(ctx_size):
        basis[:, i * rows : (i + 1) * rows] = jnp.exp(-rate * ((lane + i * rows) / seq_len))
    filt = matmul(weight * jnp.exp(rate * (lane / seq_len)), basis[...], (0, 0), EXACT)
    causal = iota((rows, rows), 1) >= iota((rows, rows), 0)
    taps[:, :rows] = jnp.zeros((rows, rows), BF16)
    taps[:, rows : 2 * rows] = jnp.where(causal, filt[:, :rows], 0.0).astype(BF16)
    taps[:, 2 * rows :] = filt[:, rows:].astype(BF16)

    arrived_plane(0)

    mixes = [got[s, :, :, :rows].reshape(blocks, rows) for s in range(PLANE_SEQS)]
    grads = [got[s, :, :, rows:].reshape(blocks, rows) for s in range(PLANE_SEQS)]
    mix_t = jnp.transpose(jnp.concatenate(mixes, axis=0))

    def shifted(k):
        if k == 0:
            return jnp.concatenate(grads, axis=0)
        gap = jnp.zeros((k * GROUP_SIZE, rows), BF16)
        return jnp.concatenate([x for a in grads for x in (a[k * GROUP_SIZE :], gap)], axis=0)

    for k in range(0, ctx_size, 2):
        pair = jnp.concatenate([shifted(k), shifted(k + 1)], axis=1)
        lags[:, k * rows : (k + 2) * rows] = matmul(mix_t, pair)
    width = seq_len + rows
    lags[:, seq_len:] = jnp.zeros((rows, rows), F32)
    parts = [lags[a * 8 : (a + 1) * 8, :] for a in range(rows // 8)]
    shift = 8
    while len(parts) > 1:
        parts = [
            parts[a] + pltpu.roll(parts[a + 1], width - shift, 1) for a in range(0, len(parts), 2)
        ]
        shift *= 2
    skew = parts[0]
    row = iota((8, width), 0)
    for bit in (1, 2, 4):
        skew = jnp.where(row & bit != 0, pltpu.roll(skew, width - bit, 1), skew)
    corr = jnp.sum(skew, axis=0, keepdims=True)
    modal = jnp.zeros((modes, rows), F32)
    direct = jnp.zeros((GROUP_SIZE, rows), F32)
    for i in range(ctx_size):
        span = slice(i * rows, (i + 1) * rows)
        modal = modal + basis[:, span] * corr[:, span]
        for s in range(PLANE_SEQS):
            direct = direct + got[s, i, :, :rows].astype(F32) * got[s, i, :, rows:].astype(F32)
    stack = jnp.concatenate(
        [modal, direct, jnp.zeros((rows - modes - GROUP_SIZE, rows), F32)], axis=0
    )
    term_send[:, :seq_len] = corr[:, :seq_len]
    term_send[:, seq_len:] = matmul(jnp.ones((8, rows), F32), stack, (1, 1), EXACT)[:1]
    term_got[level] = term_send[...]
    over_column(lambda target: push(term_send, term_got.at[level], 1, target))

    pairs = ctx_size // 2
    wide = [
        jnp.concatenate([got[s, 2 * p], got[s, 2 * p + 1]], axis=1)
        for p in range(pairs)
        for s in range(PLANE_SEQS)
    ]
    wide = jnp.concatenate(wide, axis=0)
    mix = jnp.concatenate([wide[:, :rows], wide[:, 2 * rows : 3 * rows]], axis=1)
    grad = jnp.concatenate([wide[:, rows : 2 * rows], wide[:, 3 * rows :]], axis=1)
    step = PLANE_SEQS * GROUP_SIZE
    state = jnp.zeros((pairs * step, 2 * rows), F32)
    prior = jnp.zeros((pairs * step, 2 * rows), F32)
    for q in range(pairs):
        block = jnp.concatenate(
            [
                taps[:, (2 * q + 1) * rows : (2 * q + 3) * rows],
                taps[:, 2 * q * rows : (2 * q + 2) * rows],
            ],
            axis=0,
        )
        cut = q * step
        ahead = matmul(mix[: pairs * step - cut], block)
        behind = matmul(grad[cut:], block, (1, 1))
        if q == 0:
            state, prior = ahead, behind
        else:
            gap = jnp.zeros((cut, 2 * rows), F32)
            state = state + jnp.concatenate([gap, ahead], axis=0)
            prior = prior + jnp.concatenate([behind, gap], axis=0)
    state = state.astype(BF16)
    prior = prior.astype(BF16)
    for s in range(PLANE_SEQS):
        for i in range(ctx_size):
            first_row = (i // 2) * step + s * GROUP_SIZE
            at = slice(first_row, first_row + GROUP_SIZE)
            span = slice((i % 2) * rows, (i % 2 + 1) * rows)
            back_send[s, i, :, :rows] = state[at, span]
            back_send[s, i, :, rows:] = prior[at, span]
    back_got[channels_of(plane_index)] = back_send[plane_seq, ctx_index]
    over_plane(
        lambda p, s, k, target: push(
            back_send.at[s, k], back_got.at[channels_of(plane_index)], 2, target
        )
    )

    arrived(term_got.at[pl.ds(0, depth - 1)], 1)
    total = term_got[0]
    for i in range(1, depth):
        total = total + term_got[i]
    filter_scale = 1.0 / math.sqrt(data_size * seq_len * GROUP_SIZE)
    at = iota((1, rows), 1)
    small_scale = jnp.where(
        at < modes, filter_scale / math.sqrt(seq_len), 1.0 / math.sqrt(data_size * seq_len)
    )
    small = total[:, seq_len:] * small_scale
    for i in range(ctx_size):
        sum_send[i, :, :rows] = total[:, i * rows : (i + 1) * rows] * filter_scale
        sum_send[i, :, rows:] = small
    sum_got[plane_index] = sum_send[ctx_index]
    over_plane(lambda p, s, k, target: push(sum_send.at[k], sum_got.at[plane_index], 3, target))

    arrived_plane(2)
    results = matmul(unsort[...], back_got[...])
    wide_gate = gate_out[...].astype(F32)
    wide_cot = cotangent[...].astype(F32)
    wide_in = gate_in[...].astype(F32)
    wide_signal = signal[...].astype(F32)
    mixed_wide = (wide_in * wide_signal).astype(BF16).astype(F32)
    back_wide = (wide_cot * wide_gate).astype(BF16).astype(F32)
    mixture = results[:, :rows] + bias_wide[...] * mixed_wide
    conv_out[...] = (wide_gate * mixture).astype(BF16)
    grad_gate_out[...] = (wide_cot * mixture).astype(BF16)
    grad_mixed = results[:, rows:] + bias_wide[...] * back_wide
    grad_gate_in[...] = (grad_mixed * wide_signal).astype(BF16)
    grad_signal[...] = (grad_mixed * wide_in).astype(BF16)

    for store in stores[:4]:
        store.start()

    arrived(sum_got.at[pl.ds(0, groups - 1)], 3)
    for g in range(groups):
        final[g : g + 1, :] = sum_got[g]
    grad_filter[...] = final[:, :rows]
    small = final[:, rows:]
    eye = jnp.where(iota((groups, groups), 0) == iota((groups, groups), 1), 1.0, 0.0)
    grad_residue[...] = matmul(small, eye, (0, 0), EXACT)[:modes]
    spread = matmul(small, jnp.where(member, 1.0, 0.0), (0, 0), EXACT)
    hit = iota((rows, channels), 0).astype(F32) == ranks[...] + modes
    grad_bias[...] = jnp.sum(jnp.where(hit, spread, 0.0), axis=0, keepdims=True)

    for store in stores[4:]:
        store.start()
    for store in stores:
        store.wait()
    sent(sorted_in.at[pl.ds(0, channels - GROUP_SIZE)], 0)
    sent(term_got.at[pl.ds(0, depth - 1)], 1)
    sent(back_got.at[pl.ds(0, channels - GROUP_SIZE)], 2)
    sent(sum_got.at[pl.ds(0, groups - 1)], 3)


def store_kernel(count, *refs):
    sources, results, stages = refs[:count], refs[count : 2 * count], refs[2 * count : 3 * count]
    load_sems, store_sems = refs[3 * count :]
    loads = [
        pltpu.make_async_copy(src, stage, load_sems.at[i])
        for i, (src, stage) in enumerate(zip(sources, stages))
    ]
    stores = [
        pltpu.make_async_copy(stage, dst, store_sems.at[i])
        for i, (stage, dst) in enumerate(zip(stages, results))
    ]
    for load in loads:
        load.start()
    for load, store in zip(loads, stores):
        load.wait()
        store.start()
    for store in stores:
        store.wait()


def body(gate_out, gate_in, signal, cotangent, residue, decay, skip_bias, channel_group):
    data_size = lax.axis_size("dp")
    ctx_size = lax.axis_size("ctx")
    _, channels, rows = gate_out.shape
    groups, modes = residue.shape
    depth = data_size // PLANE_SEQS
    seq_len = rows * ctx_size
    hbm = pl.BlockSpec(memory_space=pltpu.HBM)
    wide = jax.ShapeDtypeStruct((channels, rows), BF16)
    flat = lambda a: a.reshape(channels, rows)
    shapes = [
        wide,
        wide,
        wide,
        wide,
        jax.ShapeDtypeStruct((groups, rows), F32),
        jax.ShapeDtypeStruct((modes, groups), F32),
        jax.ShapeDtypeStruct((1, channels), F32),
    ]
    results = pl.pallas_call(
        functools.partial(kernel, data_size, ctx_size),
        out_shape=shapes,
        in_specs=[hbm] * 8,
        out_specs=[hbm] * len(shapes),
        scratch_shapes=[
            pltpu.VMEM((channels, rows), BF16),
            pltpu.VMEM((channels, rows), BF16),
            pltpu.VMEM((channels, rows), BF16),
            pltpu.VMEM((channels, rows), BF16),
            pltpu.VMEM((modes, groups), F32),
            pltpu.VMEM((modes, groups), F32),
            pltpu.VMEM((1, channels), F32),
            pltpu.VMEM((1, channels), jnp.int32),
            pltpu.SemaphoreType.DMA((8,)),
            *[pltpu.VMEM(a.shape, a.dtype) for a in shapes],
            pltpu.SemaphoreType.DMA((len(shapes),)),
            pltpu.VMEM((channels, 2 * rows), BF16),
            pltpu.VMEM((PLANE_SEQS, ctx_size, GROUP_SIZE, 2 * rows), BF16),
            pltpu.VMEM((channels, channels), BF16),
            pltpu.VMEM((channels, rows), F32),
            pltpu.VMEM((1, channels), F32),
            pltpu.VMEM((modes, seq_len), F32),
            pltpu.VMEM((rows, seq_len + rows), BF16),
            pltpu.VMEM((rows, seq_len + rows), F32),
            pltpu.VMEM((1, seq_len + rows), F32),
            pltpu.VMEM((depth, 1, seq_len + rows), F32),
            pltpu.VMEM((PLANE_SEQS, ctx_size, GROUP_SIZE, 2 * rows), BF16),
            pltpu.VMEM((channels, 2 * rows), BF16),
            pltpu.VMEM((ctx_size, 1, 2 * rows), F32),
            pltpu.VMEM((groups, 1, 2 * rows), F32),
            pltpu.VMEM((groups, 2 * rows), F32),
            pltpu.SemaphoreType.DMA((4,)),
            pltpu.SemaphoreType.DMA((4,)),
        ],
        compiler_params=pltpu.CompilerParams(
            collective_id=0, has_side_effects=True, vmem_limit_bytes=62 * 1024 * 1024
        ),
        cost_estimate=pl.CostEstimate(
            flops=2 * 400_000_000, bytes_accessed=2_000_000, transcendentals=100_000
        ),
    )(
        flat(gate_out),
        flat(gate_in),
        flat(signal),
        flat(cotangent),
        residue.T,
        decay.T,
        skip_bias.reshape(1, channels),
        channel_group.reshape(1, channels),
    )
    results = pl.pallas_call(
        functools.partial(store_kernel, len(shapes)),
        out_shape=shapes,
        in_specs=[hbm] * len(shapes),
        out_specs=[hbm] * len(shapes),
        scratch_shapes=[
            *[pltpu.VMEM(a.shape, a.dtype) for a in shapes],
            pltpu.SemaphoreType.DMA((len(shapes),)),
            pltpu.SemaphoreType.DMA((len(shapes),)),
        ],
    )(*results)
    lifted = tuple(a.reshape(1, channels, rows) for a in results[:4])
    return lifted + (results[4], results[5].T, results[6].reshape(channels))


def solution(mesh):
    return jax.shard_map(
        body,
        mesh=mesh,
        in_specs=(
            P("dp", None, "ctx"),
            P("dp", None, "ctx"),
            P("dp", None, "ctx"),
            P("dp", None, "ctx"),
            P(),
            P(),
            P(),
            P(),
        ),
        out_specs=(
            P("dp", None, "ctx"),
            P("dp", None, "ctx"),
            P("dp", None, "ctx"),
            P("dp", None, "ctx"),
            P(None, "ctx"),
            P(),
            P(),
        ),
        check_vma=False,
    )
```

time: 56.6 us -> 42.7 us (0.75); the launches traced: 55.6 us -> 42.6 us
  local copies, waits for them, and re-layouts: 10.2 us -> 0 us
  Pallas kernels: 44.8 us -> 42 us
    unnamed x25 -> x0, local copies, waits for them, and re-layouts: 10.2 us -> none
    pallas_call x1, Pallas kernels: 44.8 us -> 40.1 us  [body(): pl.pallas_call(functools.partial(kernel, data_size, ctx_size), out_shape=...]
    pallas_call x0 -> x1, Pallas kernels: none -> 1.88 us  [body(): pl.pallas_call(functools.partial(store_kernel, len(shapes)), out_shape=sh...]
where the time goes in v2:
time: 42.7 us; the launch traced here: 42.6 us
  Pallas kernels  42 us (98%)
  between operations  0.64 us (1%)
    pallas_call x1, Pallas kernels, body(): pl.pallas_call(functools.partial(kernel, data_size, ctx_size), out_shape=...  40.1 us
    pallas_call x1, Pallas kernels, body(): pl.pallas_call(functools.partial(store_kernel, len(shapes)), out_shape=sh...  1.88 us

profile of v2, /device:TPU:1, one launch (start us, length us, event | category | flops | bytes accessed | tf_op | source)
XLA Modules:
  0.0 42.6 jit_solution(7350979492881134462)
XLA Ops:
  0.6 40.1 %shard_map.135 = (bf16[512,128]{1,0:T(8,128)(2,1)}, bf16[512,128]{1,0:T(8,128)(2,1)}, bf16[512,128]{1,0:T(8,128)(2,1)}, bf16[512,128]{1,0:T(8,128)(2,1)}, f32[32...) custom-call(bf16[512,128]{1,0:T(8,128)(2,1)} %bitcast.14, bf16[512,128]{1,0:T(8,128)(2,1)} %bitcast.15, ...), custom_call_target="tpu_custom_call" | custom-call | flops 800000000 | bytes 2000000 | tf_op jit(solution)/shard_map/pallas_call | solution.py:408
  40.7 1.9 %shard_map.136 = (bf16[512,128]{1,0:T(8,128)(2,1)}, bf16[512,128]{1,0:T(8,128)(2,1)}, bf16[512,128]{1,0:T(8,128)(2,1)}, bf16[512,128]{1,0:T(8,128)(2,1)}, f32[32...) custom-call(bf16[512,128]{1,0:T(8,128)(2,1)} %get-tuple-element.21.refs_0_, ...), custom_call_target="tpu_custom_call" | custom-call | tf_op jit(solution)/shard_map/pallas_call | solution.py:459

commit v3 on v2

--- a/solution.py
+++ b/solution.py
@@ -82,6 +82,8 @@
     final,
     send_sems,
     recv_sems,
+    plane_ready,
+    levels_ready,
 ):
     modes, groups = residue.shape
     channels, rows = gate_out.shape
@@ -93,23 +95,30 @@
     level = lax.axis_index("dp") % depth
     plane_index = plane_seq * ctx_size + ctx_index
 
+    wide_y = ctx_size // 4
+    here = (ctx_index // 4, 2 * (lax.rem(ctx_index, 4) // 2) + plane_seq, lax.rem(ctx_index, 2))
+
+    def offset(i):
+        return jnp.where(i == 2, 3, jnp.where(i == 3, 0, 2 - i))
+
     def over_plane(step):
-        def one(o, c):
-            peer = lax.rem(plane_index + o, groups)
-            seq = peer // ctx_size
-            rank = peer - seq * ctx_size
-            step(peer, seq, rank, {"dp": seq * depth + level, "ctx": rank})
+        def one(i, c):
+            y = lax.rem(here[0] + offset(i // 8 + 4 - wide_y), wide_y)
+            x = lax.rem(here[1] + offset(lax.rem(i // 2, 4)), 4)
+            rank = 4 * y + 2 * (x // 2) + lax.rem(here[2] + 1 + i, 2)
+            seq = lax.rem(x, 2)
+            step(seq * ctx_size + rank, seq, rank, {"dp": seq * depth + level, "ctx": rank})
             return c
 
-        lax.fori_loop(1, groups, one, 0)
+        lax.fori_loop(0, groups - 1, one, 0)
 
     def over_column(step):
-        def one(o, c):
-            peer = lax.rem(level + o, depth)
-            step({"dp": plane_seq * depth + peer})
+        def one(i, c):
+            o = depth // 2 + (i + 1) // 2 * (1 - 2 * lax.rem(i, 2))
+            step({"dp": plane_seq * depth + lax.rem(level + o, depth)})
             return c
 
-        lax.fori_loop(1, depth, one, 0)
+        lax.fori_loop(0, depth - 1, one, 0)
 
     def push(src, dst, phase, target):
         pltpu.make_async_remote_copy(
@@ -164,13 +173,22 @@
     ]
 
     barrier = pltpu.get_barrier_semaphore()
-    over_plane(
-        lambda p, s, k, target: pl.semaphore_signal(
-            barrier, inc=1, device_id=target, device_id_type=MESH
+    core = lax.rem(ctx_index, 2)
+    mate = {"ctx": ctx_index + 1 - 2 * core}
+
+    def greet_plane(p, s, k, target):
+        @pl.when(lax.rem(k, 2) == 0)
+        def _():
+            pl.semaphore_signal(barrier, inc=1, device_id=target, device_id_type=MESH)
+
+    over_plane(greet_plane)
+    over_column(
+        lambda target: pl.semaphore_signal(
+            barrier,
+            inc=1,
+            device_id={"dp": target["dp"], "ctx": ctx_index + 1 - core},
+            device_id_type=MESH,
         )
-    )
-    over_column(
-        lambda target: pl.semaphore_signal(barrier, inc=1, device_id=target, device_id_type=MESH)
     )
 
     loads[0].wait()
@@ -196,7 +214,15 @@
 
     got[plane_seq, ctx_index] = sorted_in[channels_of(plane_index)]
 
-    pl.semaphore_wait(barrier, groups - 1 + depth - 1)
+    @pl.when(core == 0)
+    def _():
+        pl.semaphore_wait(barrier, groups - 1)
+        pl.semaphore_signal(plane_ready, inc=1, device_id=mate, device_id_type=MESH)
+
+    @pl.when(core == 1)
+    def _():
+        pl.semaphore_wait(plane_ready, 1)
+
     over_plane(
         lambda p, s, k, target: push(
             sorted_in.at[channels_of(p)], got.at[plane_seq, ctx_index], 0, target
@@ -221,6 +247,11 @@
     taps[:, :rows] = jnp.zeros((rows, rows), BF16)
     taps[:, rows : 2 * rows] = jnp.where(causal, filt[:, :rows], 0.0).astype(BF16)
     taps[:, 2 * rows :] = filt[:, rows:].astype(BF16)
+
+    @pl.when(core == 1)
+    def _():
+        pl.semaphore_wait(barrier, 2 * (depth - 1))
+        pl.semaphore_signal(levels_ready, inc=1, device_id=mate, device_id_type=MESH)
 
     arrived_plane(0)
 
@@ -264,6 +295,11 @@
     term_send[:, :seq_len] = corr[:, :seq_len]
     term_send[:, seq_len:] = matmul(jnp.ones((8, rows), F32), stack, (1, 1), EXACT)[:1]
     term_got[level] = term_send[...]
+
+    @pl.when(core == 0)
+    def _():
+        pl.semaphore_wait(levels_ready, 1)
+
     over_column(lambda target: push(term_send, term_got.at[level], 1, target))
 
     pairs = ctx_size // 2
@@ -439,6 +475,8 @@
             pltpu.VMEM((groups, 2 * rows), F32),
             pltpu.SemaphoreType.DMA((4,)),
             pltpu.SemaphoreType.DMA((4,)),
+            pltpu.SemaphoreType.REGULAR,
+            pltpu.SemaphoreType.REGULAR,
         ],
         compiler_params=pltpu.CompilerParams(
             collective_id=0, has_side_effects=True, vmem_limit_bytes=62 * 1024 * 1024

time: 42.7 us -> 41.3 us (0.967)
  Pallas kernels: 42 us -> 40.6 us
    pallas_call x1, Pallas kernels: 40.1 us -> 38.7 us  [body(): pl.pallas_call(functools.partial(kernel, data_size, ctx_size), out_shape=...]
where the time goes in v3:
time: 41.3 us; the launch traced here: 41.2 us
  Pallas kernels  40.6 us (98%)
  between operations  0.64 us (2%)
    pallas_call x1, Pallas kernels, body(): pl.pallas_call(functools.partial(kernel, data_size, ctx_size), out_shape=...  38.7 us
    pallas_call x1, Pallas kernels, body(): pl.pallas_call(functools.partial(store_kernel, len(shapes)), out_shape=sh...  1.88 us

profile of v3, /device:TPU:1, one launch (start us, length us, event | category | flops | bytes accessed | tf_op | source)
XLA Modules:
  0.0 41.2 jit_solution(6003901813395190983)
XLA Ops:
  0.6 38.7 %shard_map.135 = (bf16[512,128]{1,0:T(8,128)(2,1)}, bf16[512,128]{1,0:T(8,128)(2,1)}, bf16[512,128]{1,0:T(8,128)(2,1)}, bf16[512,128]{1,0:T(8,128)(2,1)}, f32[32...) custom-call(bf16[512,128]{1,0:T(8,128)(2,1)} %bitcast.14, bf16[512,128]{1,0:T(8,128)(2,1)} %bitcast.15, ...), custom_call_target="tpu_custom_call" | custom-call | flops 800000000 | bytes 2000000 | tf_op jit(solution)/shard_map/pallas_call | solution.py:444
  39.3 1.9 %shard_map.136 = (bf16[512,128]{1,0:T(8,128)(2,1)}, bf16[512,128]{1,0:T(8,128)(2,1)}, bf16[512,128]{1,0:T(8,128)(2,1)}, bf16[512,128]{1,0:T(8,128)(2,1)}, f32[32...) custom-call(bf16[512,128]{1,0:T(8,128)(2,1)} %get-tuple-element.21.refs_0_, ...), custom_call_target="tpu_custom_call" | custom-call | tf_op jit(solution)/shard_map/pallas_call | solution.py:497

commit v4 on v3

--- a/solution.py
+++ b/solution.py
@@ -41,13 +41,13 @@
     decay_hbm,
     skip_bias_hbm,
     channel_group_hbm,
-    conv_out_hbm,
-    grad_gate_out_hbm,
-    grad_gate_in_hbm,
-    grad_signal_hbm,
-    grad_filter_hbm,
-    grad_residue_hbm,
-    grad_bias_hbm,
+    conv_out,
+    grad_gate_out,
+    grad_gate_in,
+    grad_signal,
+    grad_filter,
+    grad_residue,
+    grad_bias,
     gate_out,
     gate_in,
     signal,
@@ -57,14 +57,6 @@
     skip_bias,
     channel_group,
     load_sems,
-    conv_out,
-    grad_gate_out,
-    grad_gate_in,
-    grad_signal,
-    grad_filter,
-    grad_residue,
-    grad_bias,
-    store_sems,
     sorted_in,
     got,
     unsort,
@@ -73,8 +65,11 @@
     basis,
     taps,
     lags,
+    lag_rows,
     term_send,
     term_got,
+    small_send,
+    small_got,
     back_send,
     back_got,
     sum_send,
@@ -157,20 +152,6 @@
     ]
     for load in loads:
         load.start()
-    stores = [
-        pltpu.make_async_copy(src, dst, store_sems.at[i])
-        for i, (src, dst) in enumerate(
-            [
-                (conv_out, conv_out_hbm),
-                (grad_gate_out, grad_gate_out_hbm),
-                (grad_gate_in, grad_gate_in_hbm),
-                (grad_signal, grad_signal_hbm),
-                (grad_filter, grad_filter_hbm),
-                (grad_residue, grad_residue_hbm),
-                (grad_bias, grad_bias_hbm),
-            ]
-        )
-    ]
 
     barrier = pltpu.get_barrier_semaphore()
     core = lax.rem(ctx_index, 2)
@@ -287,20 +268,27 @@
     for i in range(ctx_size):
         span = slice(i * rows, (i + 1) * rows)
         modal = modal + basis[:, span] * corr[:, span]
+        lag_rows[i : i + 1, :] = corr[:, span]
         for s in range(PLANE_SEQS):
             direct = direct + got[s, i, :, :rows].astype(F32) * got[s, i, :, rows:].astype(F32)
     stack = jnp.concatenate(
         [modal, direct, jnp.zeros((rows - modes - GROUP_SIZE, rows), F32)], axis=0
     )
-    term_send[:, :seq_len] = corr[:, :seq_len]
-    term_send[:, seq_len:] = matmul(jnp.ones((8, rows), F32), stack, (1, 1), EXACT)[:1]
+    term_send[...] = lag_rows[...].astype(BF16)
+    small_send[...] = matmul(jnp.ones((8, rows), F32), stack, (1, 1), EXACT)[:1]
     term_got[level] = term_send[...]
+    small_got[level] = small_send[...]
 
     @pl.when(core == 0)
     def _():
         pl.semaphore_wait(levels_ready, 1)
 
-    over_column(lambda target: push(term_send, term_got.at[level], 1, target))
+
+    def push_terms(target):
+        push(term_send, term_got.at[level], 1, target)
+        push(small_send, small_got.at[level], 4, target)
+
+    over_column(push_terms)
 
     pairs = ctx_size // 2
     wide = [
@@ -348,17 +336,22 @@
     )
 
     arrived(term_got.at[pl.ds(0, depth - 1)], 1)
-    total = term_got[0]
+    total = term_got[0].astype(F32)
     for i in range(1, depth):
-        total = total + term_got[i]
+        total = total + term_got[i].astype(F32)
+    arrived(small_got.at[pl.ds(0, depth - 1)], 4)
+    small = small_got[0]
+    for i in range(1, depth):
+        small = small + small_got[i]
     filter_scale = 1.0 / math.sqrt(data_size * seq_len * GROUP_SIZE)
     at = iota((1, rows), 1)
     small_scale = jnp.where(
         at < modes, filter_scale / math.sqrt(seq_len), 1.0 / math.sqrt(data_size * seq_len)
     )
-    small = total[:, seq_len:] * small_scale
+    small = small * small_scale
+    total = total * filter_scale
     for i in range(ctx_size):
-        sum_send[i, :, :rows] = total[:, i * rows : (i + 1) * rows] * filter_scale
+        sum_send[i, :, :rows] = total[i : i + 1]
         sum_send[i, :, rows:] = small
     sum_got[plane_index] = sum_send[ctx_index]
     over_plane(lambda p, s, k, target: push(sum_send.at[k], sum_got.at[plane_index], 3, target))
@@ -378,45 +371,39 @@
     grad_gate_in[...] = (grad_mixed * wide_signal).astype(BF16)
     grad_signal[...] = (grad_mixed * wide_in).astype(BF16)
 
-    for store in stores[:4]:
-        store.start()
-
     arrived(sum_got.at[pl.ds(0, groups - 1)], 3)
     for g in range(groups):
         final[g : g + 1, :] = sum_got[g]
     grad_filter[...] = final[:, :rows]
-    small = final[:, rows:]
-    eye = jnp.where(iota((groups, groups), 0) == iota((groups, groups), 1), 1.0, 0.0)
-    grad_residue[...] = matmul(small, eye, (0, 0), EXACT)[:modes]
-    spread = matmul(small, jnp.where(member, 1.0, 0.0), (0, 0), EXACT)
-    hit = iota((rows, channels), 0).astype(F32) == ranks[...] + modes
+    small = jnp.transpose(final[:, rows:])
+    grad_residue[...] = small[:modes]
+    terms = small[modes : modes + GROUP_SIZE]
+    upper = terms.astype(BF16)
+    middle = (terms - upper.astype(F32)).astype(BF16)
+    lower = (terms - upper.astype(F32) - middle.astype(F32)).astype(BF16)
+    spread = matmul(
+        jnp.concatenate([upper, middle, lower], axis=0), jnp.where(member, 1.0, 0.0).astype(BF16)
+    )
+    spread = (
+        spread[:GROUP_SIZE] + spread[GROUP_SIZE : 2 * GROUP_SIZE] + spread[2 * GROUP_SIZE :]
+    )
+    hit = iota((GROUP_SIZE, channels), 0).astype(F32) == ranks[...]
     grad_bias[...] = jnp.sum(jnp.where(hit, spread, 0.0), axis=0, keepdims=True)
 
-    for store in stores[4:]:
-        store.start()
-    for store in stores:
-        store.wait()
     sent(sorted_in.at[pl.ds(0, channels - GROUP_SIZE)], 0)
     sent(term_got.at[pl.ds(0, depth - 1)], 1)
+    sent(small_got.at[pl.ds(0, depth - 1)], 4)
     sent(back_got.at[pl.ds(0, channels - GROUP_SIZE)], 2)
     sent(sum_got.at[pl.ds(0, groups - 1)], 3)
 
 
 def store_kernel(count, *refs):
-    sources, results, stages = refs[:count], refs[count : 2 * count], refs[2 * count : 3 * count]
-    load_sems, store_sems = refs[3 * count :]
-    loads = [
-        pltpu.make_async_copy(src, stage, load_sems.at[i])
-        for i, (src, stage) in enumerate(zip(sources, stages))
+    sources, results, sems = refs[:count], refs[count : 2 * count], refs[2 * count]
+    stores = [
+        pltpu.make_async_copy(src, dst, sems.at[i])
+        for i, (src, dst) in enumerate(zip(sources, results))
     ]
-    stores = [
-        pltpu.make_async_copy(stage, dst, store_sems.at[i])
-        for i, (stage, dst) in enumerate(zip(stages, results))
-    ]
-    for load in loads:
-        load.start()
-    for load, store in zip(loads, stores):
-        load.wait()
+    for store in stores:
         store.start()
     for store in stores:
         store.wait()
@@ -429,6 +416,7 @@
     groups, modes = residue.shape
     depth = data_size // PLANE_SEQS
     seq_len = rows * ctx_size
+    vmem = pl.BlockSpec(memory_space=pltpu.VMEM)
     hbm = pl.BlockSpec(memory_space=pltpu.HBM)
     wide = jax.ShapeDtypeStruct((channels, rows), BF16)
     flat = lambda a: a.reshape(channels, rows)
@@ -443,9 +431,9 @@
     ]
     results = pl.pallas_call(
         functools.partial(kernel, data_size, ctx_size),
-        out_shape=shapes,
+        out_shape=[pltpu.VMEM(a.shape, a.dtype) for a in shapes],
         in_specs=[hbm] * 8,
-        out_specs=[hbm] * len(shapes),
+        out_specs=[vmem] * len(shapes),
         scratch_shapes=[
             pltpu.VMEM((channels, rows), BF16),
             pltpu.VMEM((channels, rows), BF16),
@@ -456,8 +444,6 @@
             pltpu.VMEM((1, channels), F32),
             pltpu.VMEM((1, channels), jnp.int32),
             pltpu.SemaphoreType.DMA((8,)),
-            *[pltpu.VMEM(a.shape, a.dtype) for a in shapes],
-            pltpu.SemaphoreType.DMA((len(shapes),)),
             pltpu.VMEM((channels, 2 * rows), BF16),
             pltpu.VMEM((PLANE_SEQS, ctx_size, GROUP_SIZE, 2 * rows), BF16),
             pltpu.VMEM((channels, channels), BF16),
@@ -466,44 +452,47 @@
             pltpu.VMEM((modes, seq_len), F32),
             pltpu.VMEM((rows, seq_len + rows), BF16),
             pltpu.VMEM((rows, seq_len + rows), F32),
-            pltpu.VMEM((1, seq_len + rows), F32),
-            pltpu.VMEM((depth, 1, seq_len + rows), F32),
+            pltpu.VMEM((ctx_size, rows), F32),
+            pltpu.VMEM((ctx_size, rows), BF16),
+            pltpu.VMEM((depth, ctx_size, rows), BF16),
+            pltpu.VMEM((1, rows), F32),
+            pltpu.VMEM((depth, 1, rows), F32),
             pltpu.VMEM((PLANE_SEQS, ctx_size, GROUP_SIZE, 2 * rows), BF16),
             pltpu.VMEM((channels, 2 * rows), BF16),
             pltpu.VMEM((ctx_size, 1, 2 * rows), F32),
             pltpu.VMEM((groups, 1, 2 * rows), F32),
             pltpu.VMEM((groups, 2 * rows), F32),
-            pltpu.SemaphoreType.DMA((4,)),
-            pltpu.SemaphoreType.DMA((4,)),
+            pltpu.SemaphoreType.DMA((5,)),
+            pltpu.SemaphoreType.DMA((5,)),
             pltpu.SemaphoreType.REGULAR,
             pltpu.SemaphoreType.REGULAR,
         ],
         compiler_params=pltpu.CompilerParams(
-            collective_id=0, has_side_effects=True, vmem_limit_bytes=62 * 1024 * 1024
+            collective_id=0, has_side_effects=True, vmem_limit_bytes=32 * 1024 * 1024
         ),
         cost_estimate=pl.CostEstimate(
             flops=2 * 400_000_000, bytes_accessed=2_000_000, transcendentals=100_000
         ),
-    )(
-        flat(gate_out),
-        flat(gate_in),
-        flat(signal),
-        flat(cotangent),
-        residue.T,
-        decay.T,
-        skip_bias.reshape(1, channels),
-        channel_group.reshape(1, channels),
-    )
+    )(*[
+        pltpu.with_memory_space_constraint(a, pltpu.HBM)
+        for a in (
+            flat(gate_out),
+            flat(gate_in),
+            flat(signal),
+            flat(cotangent),
+            residue.T,
+            decay.T,
+            skip_bias.reshape(1, channels),
+            channel_group.reshape(1, channels),
+        )
+    ])
     results = pl.pallas_call(
         functools.partial(store_kernel, len(shapes)),
         out_shape=shapes,
-        in_specs=[hbm] * len(shapes),
+        in_specs=[vmem] * len(shapes),
         out_specs=[hbm] * len(shapes),
-        scratch_shapes=[
-            *[pltpu.VMEM(a.shape, a.dtype) for a in shapes],
-            pltpu.SemaphoreType.DMA((len(shapes),)),
-            pltpu.SemaphoreType.DMA((len(shapes),)),
-        ],
+        scratch_shapes=[pltpu.SemaphoreType.DMA((len(shapes),))],
+        compiler_params=pltpu.CompilerParams(vmem_limit_bytes=4 * 1024 * 1024),
     )(*results)
     lifted = tuple(a.reshape(1, channels, rows) for a in results[:4])
     return lifted + (results[4], results[5].T, results[6].reshape(channels))

time: 41.3 us -> 37.6 us (0.910)
  Pallas kernels: 40.6 us -> 36.8 us
    pallas_call x1, Pallas kernels: 38.7 us -> 36 us  [body(): pl.pallas_call(functools.partial(kernel, data_size, ctx_size), out_shape=...]
    pallas_call x1, Pallas kernels: 1.88 us -> 0.86 us  [body(): pl.pallas_call(functools.partial(store_kernel, len(shapes)), out_shape=sh...]
where the time goes in v4:
time: 37.6 us; the launch traced here: 37.5 us
  Pallas kernels  36.8 us (98%)
  between operations  0.64 us (2%)
    pallas_call x1, Pallas kernels, body(): pl.pallas_call(functools.partial(kernel, data_size, ctx_size), out_shape=...  36 us
    pallas_call x1, Pallas kernels, body(): pl.pallas_call(functools.partial(store_kernel, len(shapes)), out_shape=sh...  0.86 us

profile of v4, /device:TPU:1, one launch (start us, length us, event | category | flops | bytes accessed | tf_op | source)
XLA Modules:
  0.0 37.5 jit_solution(7473989013577272431)
XLA Ops:
  0.6 36.0 %shard_map.135 = (bf16[512,128]{1,0:T(8,128)(2,1)S(1)}, bf16[512,128]{1,0:T(8,128)(2,1)S(1)}, bf16[512,128]{1,0:T(8,128)(2,1)S(1)}, bf16[512,128]{1,0:T(8,128)(2...) custom-call(bf16[512,128]{1,0:T(8,128)(2,1)} %bitcast.14, bf16[512,128]{1,0:T(8,128)(2,1)} %bitcast.15, ...), custom_call_target="tpu_custom_call" | custom-call | flops 800000000 | bytes 2000000 | tf_op jit(solution)/shard_map/pallas_call | solution.py:432
  36.6 0.9 %shard_map.136 = (bf16[512,128]{1,0:T(8,128)(2,1)}, bf16[512,128]{1,0:T(8,128)(2,1)}, bf16[512,128]{1,0:T(8,128)(2,1)}, bf16[512,128]{1,0:T(8,128)(2,1)}, f32[32...) custom-call(bf16[512,128]{1,0:T(8,128)(2,1)S(1)} %get-tuple-element.21.refs_0_, ...), custom_call_target="tpu_custom_call" | custom-call | tf_op jit(solution)/shard_map/pallas_call | solution.py:489

commit v5 on v4

--- a/solution.py
+++ b/solution.py
@@ -96,16 +96,22 @@
     def offset(i):
         return jnp.where(i == 2, 3, jnp.where(i == 3, 0, 2 - i))
 
+    def visit(step, chip, side):
+        y = lax.rem(here[0] + offset(chip // 4 + 4 - wide_y), wide_y)
+        x = lax.rem(here[1] + offset(lax.rem(chip, 4)), 4)
+        rank = 4 * y + 2 * (x // 2) + side
+        seq = lax.rem(x, 2)
+        step(seq * ctx_size + rank, seq, rank, {"dp": seq * depth + level, "ctx": rank})
+
     def over_plane(step):
         def one(i, c):
-            y = lax.rem(here[0] + offset(i // 8 + 4 - wide_y), wide_y)
-            x = lax.rem(here[1] + offset(lax.rem(i // 2, 4)), 4)
-            rank = 4 * y + 2 * (x // 2) + lax.rem(here[2] + 1 + i, 2)
-            seq = lax.rem(x, 2)
-            step(seq * ctx_size + rank, seq, rank, {"dp": seq * depth + level, "ctx": rank})
+            visit(step, i // 2, lax.rem(here[2] + 1 + i, 2))
             return c
 
         lax.fori_loop(0, groups - 1, one, 0)
+
+    def over_chips(step, side, count):
+        lax.fori_loop(0, count, lambda i, c: (visit(step, i, side), c)[1], 0)
 
     def over_column(step):
         def one(i, c):
@@ -158,7 +164,7 @@
     mate = {"ctx": ctx_index + 1 - 2 * core}
 
     def greet_plane(p, s, k, target):
-        @pl.when(lax.rem(k, 2) == 0)
+        @pl.when(lax.rem(k, 2) == 1)
         def _():
             pl.semaphore_signal(barrier, inc=1, device_id=target, device_id_type=MESH)
 
@@ -167,7 +173,7 @@
         lambda target: pl.semaphore_signal(
             barrier,
             inc=1,
-            device_id={"dp": target["dp"], "ctx": ctx_index + 1 - core},
+            device_id={"dp": target["dp"], "ctx": ctx_index - core},
             device_id_type=MESH,
         )
     )
@@ -195,12 +201,12 @@
 
     got[plane_seq, ctx_index] = sorted_in[channels_of(plane_index)]
 
-    @pl.when(core == 0)
+    @pl.when(core == 1)
     def _():
         pl.semaphore_wait(barrier, groups - 1)
         pl.semaphore_signal(plane_ready, inc=1, device_id=mate, device_id_type=MESH)
 
-    @pl.when(core == 1)
+    @pl.when(core == 0)
     def _():
         pl.semaphore_wait(plane_ready, 1)
 
@@ -229,7 +235,7 @@
     taps[:, rows : 2 * rows] = jnp.where(causal, filt[:, :rows], 0.0).astype(BF16)
     taps[:, 2 * rows :] = filt[:, rows:].astype(BF16)
 
-    @pl.when(core == 1)
+    @pl.when(core == 0)
     def _():
         pl.semaphore_wait(barrier, 2 * (depth - 1))
         pl.semaphore_signal(levels_ready, inc=1, device_id=mate, device_id_type=MESH)
@@ -263,32 +269,48 @@
     for bit in (1, 2, 4):
         skew = jnp.where(row & bit != 0, pltpu.roll(skew, width - bit, 1), skew)
     corr = jnp.sum(skew, axis=0, keepdims=True)
+    for i in range(ctx_size):
+        lag_rows[i : i + 1, :] = corr[:, i * rows : (i + 1) * rows]
+    term_send[...] = lag_rows[...].astype(BF16)
+
+    @pl.when(core == 1)
+    def _():
+        pl.semaphore_wait(levels_ready, 1)
+
+    def to_column(src, dst, phase):
+        over_column(
+            lambda target: push(
+                src, dst, phase, {"dp": target["dp"], "ctx": ctx_index + 1 - core}
+            )
+        )
+
+        @pl.when(core == 0)
+        def _():
+            push(src, dst, phase, mate)
+
+    @pl.when(core == 1)
+    def _():
+        term_got[2 * level + 1] = term_send[...]
+
+    to_column(term_send, term_got.at[2 * level + core], 1)
+
     modal = jnp.zeros((modes, rows), F32)
     direct = jnp.zeros((GROUP_SIZE, rows), F32)
     for i in range(ctx_size):
         span = slice(i * rows, (i + 1) * rows)
         modal = modal + basis[:, span] * corr[:, span]
-        lag_rows[i : i + 1, :] = corr[:, span]
         for s in range(PLANE_SEQS):
             direct = direct + got[s, i, :, :rows].astype(F32) * got[s, i, :, rows:].astype(F32)
     stack = jnp.concatenate(
         [modal, direct, jnp.zeros((rows - modes - GROUP_SIZE, rows), F32)], axis=0
     )
-    term_send[...] = lag_rows[...].astype(BF16)
     small_send[...] = matmul(jnp.ones((8, rows), F32), stack, (1, 1), EXACT)[:1]
-    term_got[level] = term_send[...]
-    small_got[level] = small_send[...]
-
-    @pl.when(core == 0)
-    def _():
-        pl.semaphore_wait(levels_ready, 1)
-
-
-    def push_terms(target):
-        push(term_send, term_got.at[level], 1, target)
-        push(small_send, small_got.at[level], 4, target)
-
-    over_column(push_terms)
+
+    @pl.when(core == 1)
+    def _():
+        small_got[2 * level + 1] = small_send[...]
+
+    to_column(small_send, small_got.at[2 * level + core], 4)
 
     pairs = ctx_size // 2
     wide = [
@@ -335,26 +357,37 @@
         )
     )
 
-    arrived(term_got.at[pl.ds(0, depth - 1)], 1)
-    total = term_got[0].astype(F32)
-    for i in range(1, depth):
-        total = total + term_got[i].astype(F32)
-    arrived(small_got.at[pl.ds(0, depth - 1)], 4)
-    small = small_got[0]
-    for i in range(1, depth):
-        small = small + small_got[i]
     filter_scale = 1.0 / math.sqrt(data_size * seq_len * GROUP_SIZE)
     at = iota((1, rows), 1)
     small_scale = jnp.where(
         at < modes, filter_scale / math.sqrt(seq_len), 1.0 / math.sqrt(data_size * seq_len)
     )
-    small = small * small_scale
-    total = total * filter_scale
-    for i in range(ctx_size):
-        sum_send[i, :, :rows] = total[i : i + 1]
-        sum_send[i, :, rows:] = small
-    sum_got[plane_index] = sum_send[ctx_index]
-    over_plane(lambda p, s, k, target: push(sum_send.at[k], sum_got.at[plane_index], 3, target))
+    pair = pl.ds(plane_index - 1, 2)
+
+    @pl.when(core == 1)
+    def _():
+        arrived(term_got.at[pl.ds(0, 2 * depth - 1)], 1)
+        arrived(small_got.at[pl.ds(0, 2 * depth - 1)], 4)
+        for c in range(2):
+            total = term_got[c].astype(F32)
+            small = small_got[c]
+            for i in range(1, depth):
+                total = total + term_got[2 * i + c].astype(F32)
+                small = small + small_got[2 * i + c]
+            total = total * filter_scale
+            small = small * small_scale
+            for i in range(ctx_size):
+                sum_send[i, c, :, :rows] = total[i : i + 1]
+                sum_send[i, c, :, rows:] = small
+        sum_got[pair] = sum_send[ctx_index]
+
+        def push_sums(phase):
+            return lambda p, s, k, target: push(
+                sum_send.at[k], sum_got.at[pair], phase, target
+            )
+
+        over_chips(push_sums(3), 1, groups // 2 - 1)
+        over_chips(push_sums(5), 0, groups // 2)
 
     arrived_plane(2)
     results = matmul(unsort[...], back_got[...])
@@ -371,7 +404,14 @@
     grad_gate_in[...] = (grad_mixed * wide_signal).astype(BF16)
     grad_signal[...] = (grad_mixed * wide_in).astype(BF16)
 
-    arrived(sum_got.at[pl.ds(0, groups - 1)], 3)
+    @pl.when(core == 0)
+    def _():
+        arrived(sum_got, 5)
+
+    @pl.when(core == 1)
+    def _():
+        arrived(sum_got.at[pl.ds(0, groups - 2)], 3)
+
     for g in range(groups):
         final[g : g + 1, :] = sum_got[g]
     grad_filter[...] = final[:, :rows]
@@ -391,10 +431,19 @@
     grad_bias[...] = jnp.sum(jnp.where(hit, spread, 0.0), axis=0, keepdims=True)
 
     sent(sorted_in.at[pl.ds(0, channels - GROUP_SIZE)], 0)
-    sent(term_got.at[pl.ds(0, depth - 1)], 1)
-    sent(small_got.at[pl.ds(0, depth - 1)], 4)
     sent(back_got.at[pl.ds(0, channels - GROUP_SIZE)], 2)
-    sent(sum_got.at[pl.ds(0, groups - 1)], 3)
+
+    @pl.when(core == 0)
+    def _():
+        sent(term_got.at[pl.ds(0, depth)], 1)
+        sent(small_got.at[pl.ds(0, depth)], 4)
+
+    @pl.when(core == 1)
+    def _():
+        sent(term_got.at[pl.ds(0, depth - 1)], 1)
+        sent(small_got.at[pl.ds(0, depth - 1)], 4)
+        sent(sum_send.at[pl.ds(0, groups // 2 - 1)], 3)
+        sent(sum_send, 5)
 
 
 def store_kernel(count, *refs):
@@ -454,16 +503,16 @@
             pltpu.VMEM((rows, seq_len + rows), F32),
             pltpu.VMEM((ctx_size, rows), F32),
             pltpu.VMEM((ctx_size, rows), BF16),
-            pltpu.VMEM((depth, ctx_size, rows), BF16),
+            pltpu.VMEM((2 * depth, ctx_size, rows), BF16),
             pltpu.VMEM((1, rows), F32),
-            pltpu.VMEM((depth, 1, rows), F32),
+            pltpu.VMEM((2 * depth, 1, rows), F32),
             pltpu.VMEM((PLANE_SEQS, ctx_size, GROUP_SIZE, 2 * rows), BF16),
             pltpu.VMEM((channels, 2 * rows), BF16),
-            pltpu.VMEM((ctx_size, 1, 2 * rows), F32),
+            pltpu.VMEM((ctx_size, 2, 1, 2 * rows), F32),
             pltpu.VMEM((groups, 1, 2 * rows), F32),
             pltpu.VMEM((groups, 2 * rows), F32),
-            pltpu.SemaphoreType.DMA((5,)),
-            pltpu.SemaphoreType.DMA((5,)),
+            pltpu.SemaphoreType.DMA((6,)),
+            pltpu.SemaphoreType.DMA((6,)),
             pltpu.SemaphoreType.REGULAR,
             pltpu.SemaphoreType.REGULAR,
         ],

time: 37.6 us -> 37.1 us (0.987)
  Pallas kernels: 36.8 us -> 36.4 us
    pallas_call x1, Pallas kernels: 36 us -> 35.5 us  [body(): pl.pallas_call(functools.partial(kernel, data_size, ctx_size), out_shape=...]
where the time goes in v5:
time: 37.1 us; the launch traced here: 37 us
  Pallas kernels  36.4 us (98%)
  between operations  0.64 us (2%)
    pallas_call x1, Pallas kernels, body(): pl.pallas_call(functools.partial(kernel, data_size, ctx_size), out_shape=...  35.5 us
    pallas_call x1, Pallas kernels, body(): pl.pallas_call(functools.partial(store_kernel, len(shapes)), out_shape=sh...  0.86 us

profile of v5, /device:TPU:1, one launch (start us, length us, event | category | flops | bytes accessed | tf_op | source)
XLA Modules:
  0.0 37.0 jit_solution(652680106008808295)
XLA Ops:
  0.6 35.5 %shard_map.135 = (bf16[512,128]{1,0:T(8,128)(2,1)S(1)}, bf16[512,128]{1,0:T(8,128)(2,1)S(1)}, bf16[512,128]{1,0:T(8,128)(2,1)S(1)}, bf16[512,128]{1,0:T(8,128)(2...) custom-call(bf16[512,128]{1,0:T(8,128)(2,1)} %bitcast.14, bf16[512,128]{1,0:T(8,128)(2,1)} %bitcast.15, ...), custom_call_target="tpu_custom_call" | custom-call | flops 800000000 | bytes 2000000 | tf_op jit(solution)/shard_map/pallas_call | solution.py:481
  36.2 0.9 %shard_map.136 = (bf16[512,128]{1,0:T(8,128)(2,1)}, bf16[512,128]{1,0:T(8,128)(2,1)}, bf16[512,128]{1,0:T(8,128)(2,1)}, bf16[512,128]{1,0:T(8,128)(2,1)}, f32[32...) custom-call(bf16[512,128]{1,0:T(8,128)(2,1)S(1)} %get-tuple-element.21.refs_0_, ...), custom_call_target="tpu_custom_call" | custom-call | tf_op jit(solution)/shard_map/pallas_call | solution.py:538

commit v6 on v5

--- a/solution.py
+++ b/solution.py
@@ -91,35 +91,38 @@
     plane_index = plane_seq * ctx_size + ctx_index
 
     wide_y = ctx_size // 4
-    here = (ctx_index // 4, 2 * (lax.rem(ctx_index, 4) // 2) + plane_seq, lax.rem(ctx_index, 2))
-
-    def offset(i):
-        return jnp.where(i == 2, 3, jnp.where(i == 3, 0, 2 - i))
+    core = lax.rem(ctx_index, 2)
+    here_y = ctx_index // 4
+    here_x = 2 * (lax.rem(ctx_index, 4) // 2) + plane_seq
+    chips = []
+    for dy in (2, 1, 3, 0)[4 - wide_y :]:
+        y = lax.rem(here_y + dy, wide_y)
+        for dx in (2, 1, 3, 0):
+            x = lax.rem(here_x + dx, 4)
+            seq = lax.rem(x, 2)
+            chips.append((4 * y + x - seq, seq, seq * depth + level))
+    half = depth // 2
+    column = [half + (i + 1) // 2 * (1 - 2 * (i % 2)) for i in range(depth - 1)]
+    column = [plane_seq * depth + lax.rem(level + o, depth) for o in column]
 
     def visit(step, chip, side):
-        y = lax.rem(here[0] + offset(chip // 4 + 4 - wide_y), wide_y)
-        x = lax.rem(here[1] + offset(lax.rem(chip, 4)), 4)
-        rank = 4 * y + 2 * (x // 2) + side
-        seq = lax.rem(x, 2)
-        step(seq * ctx_size + rank, seq, rank, {"dp": seq * depth + level, "ctx": rank})
+        first, seq, data_rank = chip
+        rank = first + side
+        step(seq * ctx_size + rank, seq, rank, {"dp": data_rank, "ctx": rank})
 
     def over_plane(step):
-        def one(i, c):
-            visit(step, i // 2, lax.rem(here[2] + 1 + i, 2))
-            return c
-
-        lax.fori_loop(0, groups - 1, one, 0)
+        for chip in chips[:-1]:
+            visit(step, chip, 1 - core)
+            visit(step, chip, core)
+        visit(step, chips[-1], 1 - core)
 
     def over_chips(step, side, count):
-        lax.fori_loop(0, count, lambda i, c: (visit(step, i, side), c)[1], 0)
+        for chip in chips[:count]:
+            visit(step, chip, side)
 
     def over_column(step):
-        def one(i, c):
-            o = depth // 2 + (i + 1) // 2 * (1 - 2 * lax.rem(i, 2))
-            step({"dp": plane_seq * depth + lax.rem(level + o, depth)})
-            return c
-
-        lax.fori_loop(0, depth - 1, one, 0)
+        for data_rank in column:
+            step({"dp": data_rank})
 
     def push(src, dst, phase, target):
         pltpu.make_async_remote_copy(
@@ -160,15 +163,17 @@
         load.start()
 
     barrier = pltpu.get_barrier_semaphore()
-    core = lax.rem(ctx_index, 2)
     mate = {"ctx": ctx_index + 1 - 2 * core}
 
-    def greet_plane(p, s, k, target):
-        @pl.when(lax.rem(k, 2) == 1)
-        def _():
-            pl.semaphore_signal(barrier, inc=1, device_id=target, device_id_type=MESH)
-
-    over_plane(greet_plane)
+    def greet(p, s, k, target):
+        pl.semaphore_signal(barrier, inc=1, device_id=target, device_id_type=MESH)
+
+    over_chips(greet, 1, groups // 2 - 1)
+
+    @pl.when(core == 0)
+    def _():
+        pl.semaphore_signal(barrier, inc=1, device_id=mate, device_id_type=MESH)
+
     over_column(
         lambda target: pl.semaphore_signal(
             barrier,

time: 37.1 us -> 37 us (level)
  no operation moved by 1% of the time
where the time goes in v6:
time: 37 us; the launch traced here: 36.8 us
  Pallas kernels  36.2 us (98%)
  between operations  0.64 us (2%)
    pallas_call x1, Pallas kernels, body(): pl.pallas_call(functools.partial(kernel, data_size, ctx_size), out_shape=...  35.3 us
    pallas_call x1, Pallas kernels, body(): pl.pallas_call(functools.partial(store_kernel, len(shapes)), out_shape=sh...  0.86 us

profile of v6, /device:TPU:1, one launch (start us, length us, event | category | flops | bytes accessed | tf_op | source)
XLA Modules:
  0.0 36.8 jit_solution(9210185074411251969)
XLA Ops:
  0.6 35.3 %shard_map.135 = (bf16[512,128]{1,0:T(8,128)(2,1)S(1)}, bf16[512,128]{1,0:T(8,128)(2,1)S(1)}, bf16[512,128]{1,0:T(8,128)(2,1)S(1)}, bf16[512,128]{1,0:T(8,128)(2...) custom-call(bf16[512,128]{1,0:T(8,128)(2,1)} %bitcast.14, bf16[512,128]{1,0:T(8,128)(2,1)} %bitcast.15, ...), custom_call_target="tpu_custom_call" | custom-call | flops 800000000 | bytes 2000000 | tf_op jit(solution)/shard_map/pallas_call | solution.py:486
  36.0 0.9 %shard_map.136 = (bf16[512,128]{1,0:T(8,128)(2,1)}, bf16[512,128]{1,0:T(8,128)(2,1)}, bf16[512,128]{1,0:T(8,128)(2,1)}, bf16[512,128]{1,0:T(8,128)(2,1)}, f32[32...) custom-call(bf16[512,128]{1,0:T(8,128)(2,1)S(1)} %get-tuple-element.21.refs_0_, ...), custom_call_target="tpu_custom_call" | custom-call | tf_op jit(solution)/shard_map/pallas_call | solution.py:543

commit v7 on v6

--- a/solution.py
+++ b/solution.py
@@ -159,20 +159,21 @@
             ]
         )
     ]
+
+    barrier = pltpu.get_barrier_semaphore()
+    mate = {"ctx": ctx_index + 1 - 2 * core}
+
+    def greet(p, s, k, target):
+        pl.semaphore_signal(barrier, inc=1, device_id=target, device_id_type=MESH)
+
+    over_chips(greet, 1, groups // 2 - 1)
+
+    @pl.when(core == 0)
+    def _():
+        pl.semaphore_signal(barrier, inc=1, device_id=mate, device_id_type=MESH)
+
     for load in loads:
         load.start()
-
-    barrier = pltpu.get_barrier_semaphore()
-    mate = {"ctx": ctx_index + 1 - 2 * core}
-
-    def greet(p, s, k, target):
-        pl.semaphore_signal(barrier, inc=1, device_id=target, device_id_type=MESH)
-
-    over_chips(greet, 1, groups // 2 - 1)
-
-    @pl.when(core == 0)
-    def _():
-        pl.semaphore_signal(barrier, inc=1, device_id=mate, device_id_type=MESH)
 
     over_column(
         lambda target: pl.semaphore_signal(

time: 37 us -> 37 us (level)
  no operation moved by 1% of the time
where the time goes in v7:
time: 37 us; the launch traced here: 36.8 us
  Pallas kernels  36.2 us (98%)
  between operations  0.64 us (2%)
    pallas_call x1, Pallas kernels, body(): pl.pallas_call(functools.partial(kernel, data_size, ctx_size), out_shape=...  35.3 us
    pallas_call x1, Pallas kernels, body(): pl.pallas_call(functools.partial(store_kernel, len(shapes)), out_shape=sh...  0.86 us

profile of v7, /device:TPU:1, one launch (start us, length us, event | category | flops | bytes accessed | tf_op | source)
XLA Modules:
  0.0 36.8 jit_solution(15167512724138971652)
XLA Ops:
  0.6 35.3 %shard_map.135 = (bf16[512,128]{1,0:T(8,128)(2,1)S(1)}, bf16[512,128]{1,0:T(8,128)(2,1)S(1)}, bf16[512,128]{1,0:T(8,128)(2,1)S(1)}, bf16[512,128]{1,0:T(8,128)(2...) custom-call(bf16[512,128]{1,0:T(8,128)(2,1)} %bitcast.14, bf16[512,128]{1,0:T(8,128)(2,1)} %bitcast.15, ...), custom_call_target="tpu_custom_call" | custom-call | flops 800000000 | bytes 2000000 | tf_op jit(solution)/shard_map/pallas_call | solution.py:487
  36.0 0.9 %shard_map.136 = (bf16[512,128]{1,0:T(8,128)(2,1)}, bf16[512,128]{1,0:T(8,128)(2,1)}, bf16[512,128]{1,0:T(8,128)(2,1)}, bf16[512,128]{1,0:T(8,128)(2,1)}, f32[32...) custom-call(bf16[512,128]{1,0:T(8,128)(2,1)S(1)} %get-tuple-element.21.refs_0_, ...), custom_call_target="tpu_custom_call" | custom-call | tf_op jit(solution)/shard_map/pallas_call | solution.py:544

commit v8 on v6

--- a/solution.py
+++ b/solution.py
@@ -164,24 +164,34 @@
 
     barrier = pltpu.get_barrier_semaphore()
     mate = {"ctx": ctx_index + 1 - 2 * core}
+    proxy_rank = ctx_index - lax.rem(ctx_index, 4) + 2
+    on_proxy_chip = jnp.logical_and(plane_seq == 0, lax.rem(ctx_index, 4) >= 2)
+    is_proxy = jnp.logical_and(on_proxy_chip, core == 0)
+    row_size = 4 * PLANE_SEQS
 
     def greet(p, s, k, target):
         pl.semaphore_signal(barrier, inc=1, device_id=target, device_id_type=MESH)
 
-    over_chips(greet, 1, groups // 2 - 1)
-
-    @pl.when(core == 0)
+    def greet_even(p, s, k, target):
+        @pl.when(jnp.logical_or(s != 0, lax.rem(k, 4) != 2))
+        def _():
+            greet(p, s, k, target)
+
+    for chip in chips[:-1]:
+        visit(greet, chip, 1)
+        visit(greet_even, chip, 0)
+
+    @pl.when(jnp.logical_not(jnp.logical_and(on_proxy_chip, core == 1)))
     def _():
         pl.semaphore_signal(barrier, inc=1, device_id=mate, device_id_type=MESH)
 
-    over_column(
-        lambda target: pl.semaphore_signal(
+    for data_rank in column:
+        pl.semaphore_signal(
             barrier,
             inc=1,
-            device_id={"dp": target["dp"], "ctx": ctx_index - core},
+            device_id={"dp": data_rank - plane_seq * depth, "ctx": proxy_rank},
             device_id_type=MESH,
         )
-    )
 
     loads[0].wait()
     member = iota((groups, channels), 0) == channel_group[...]
@@ -206,12 +216,15 @@
 
     got[plane_seq, ctx_index] = sorted_in[channels_of(plane_index)]
 
-    @pl.when(core == 1)
+    @pl.when(jnp.logical_not(is_proxy))
     def _():
         pl.semaphore_wait(barrier, groups - 1)
+
+    @pl.when(jnp.logical_and(on_proxy_chip, core == 1))
+    def _():
         pl.semaphore_signal(plane_ready, inc=1, device_id=mate, device_id_type=MESH)
 
-    @pl.when(core == 0)
+    @pl.when(is_proxy)
     def _():
         pl.semaphore_wait(plane_ready, 1)
 
@@ -240,10 +253,22 @@
     taps[:, rows : 2 * rows] = jnp.where(causal, filt[:, :rows], 0.0).astype(BF16)
     taps[:, 2 * rows :] = filt[:, rows:].astype(BF16)
 
-    @pl.when(core == 0)
-    def _():
-        pl.semaphore_wait(barrier, 2 * (depth - 1))
-        pl.semaphore_signal(levels_ready, inc=1, device_id=mate, device_id_type=MESH)
+    @pl.when(is_proxy)
+    def _():
+        pl.semaphore_wait(barrier, row_size * (depth - 1))
+
+        def tell(i, c):
+            seq = i // 4
+            pl.semaphore_signal(
+                levels_ready,
+                inc=1,
+                device_id={"dp": seq * depth + level, "ctx": proxy_rank - 2 + lax.rem(i, 4)},
+                device_id_type=MESH,
+            )
+            return c
+
+        lax.fori_loop(0, 2, tell, 0)
+        lax.fori_loop(3, row_size, tell, 0)
 
     arrived_plane(0)
 
@@ -278,7 +303,7 @@
         lag_rows[i : i + 1, :] = corr[:, i * rows : (i + 1) * rows]
     term_send[...] = lag_rows[...].astype(BF16)
 
-    @pl.when(core == 1)
+    @pl.when(jnp.logical_not(is_proxy))
     def _():
         pl.semaphore_wait(levels_ready, 1)
 

time: 37 us -> 37 us (level)
  no operation moved by 1% of the time
where the time goes in v8:
time: 37 us; the launch traced here: 36.8 us
  Pallas kernels  36.2 us (98%)
  between operations  0.64 us (2%)
    pallas_call x1, Pallas kernels, body(): pl.pallas_call(functools.partial(kernel, data_size, ctx_size), out_shape=...  35.3 us
    pallas_call x1, Pallas kernels, body(): pl.pallas_call(functools.partial(store_kernel, len(shapes)), out_shape=sh...  0.86 us

profile of v8, /device:TPU:1, one launch (start us, length us, event | category | flops | bytes accessed | tf_op | source)
XLA Modules:
  0.0 36.8 jit_solution(5524754367275221992)
XLA Ops:
  0.6 35.3 %shard_map.135 = (bf16[512,128]{1,0:T(8,128)(2,1)S(1)}, bf16[512,128]{1,0:T(8,128)(2,1)S(1)}, bf16[512,128]{1,0:T(8,128)(2,1)S(1)}, bf16[512,128]{1,0:T(8,128)(2...) custom-call(bf16[512,128]{1,0:T(8,128)(2,1)} %bitcast.14, bf16[512,128]{1,0:T(8,128)(2,1)} %bitcast.15, ...), custom_call_target="tpu_custom_call" | custom-call | flops 800000000 | bytes 2000000 | tf_op jit(solution)/shard_map/pallas_call | solution.py:511
  36.0 0.9 %shard_map.136 = (bf16[512,128]{1,0:T(8,128)(2,1)}, bf16[512,128]{1,0:T(8,128)(2,1)}, bf16[512,128]{1,0:T(8,128)(2,1)}, bf16[512,128]{1,0:T(8,128)(2,1)}, f32[32...) custom-call(bf16[512,128]{1,0:T(8,128)(2,1)S(1)} %get-tuple-element.21.refs_0_, ...), custom_call_target="tpu_custom_call" | custom-call | tf_op jit(solution)/shard_map/pallas_call | solution.py:568
